TPU v7x, 128 devices: a whole 4x4x4 slice. The times are simulated.
128 devices in a mesh: roll: 8 (over y, core), fsdp: 16 (over x, z).
Axes of the slice: x: 4, y: 4, z: 4, core: 2. Of those that a mesh axis runs over, the one named last changes fastest.
Arguments:
- latents: bfloat16 [256, 80, 2432], P(('roll', 'fsdp')), may hold values from -6 to 6
- stale_velocity: bfloat16 [256, 80, 2432], P(('roll', 'fsdp')), may hold values from -6 to 6
- noise: bfloat16 [256, 80, 2432], P(('roll', 'fsdp')), may hold values from -6 to 6
- modulation: float32 [256, 3, 2432], P(('roll', 'fsdp')), may hold values from -3 to 3
- step_ratio: float32 [256], P(('roll', 'fsdp')), may hold values from 0.003 to 0.03
- rewards: float32 [256], P(('roll', 'fsdp')), may hold values from 0 to 1
- group_ids: int32 [256], P(('roll', 'fsdp')), may hold values from 0 to 11
- step_index: int32 [256], P(('roll', 'fsdp')), may hold values from 0 to 9
- valid_steps: int32 [256], P(('roll', 'fsdp')), may hold values from 1 to 10
- patch_mask: int32 [256, 80], P(('roll', 'fsdp')), may hold values 0 or 1
- params: float32 [2, 2432, 5120], P(None, 'fsdp', 'roll'), may hold values from -0.125 to 0.125
- first_moment: float32 [2, 2432, 5120], P(None, 'fsdp', 'roll'), may hold values from -6e-05 to 6e-05
- second_moment: float32 [2, 2432, 5120], P(None, 'fsdp', 'roll'), may hold values from 1e-11 to 1e-09
Outputs:
- new_params: float32 [2, 2432, 5120], P(None, 'fsdp', 'roll')
- new_first: float32 [2, 2432, 5120], P(None, 'fsdp', 'roll')
- new_second: float32 [2, 2432, 5120], P(None, 'fsdp', 'roll')
- rollout_weights: bfloat16 [2, 2432, 5120], P(None, 'fsdp')
All inputs are finite; a program needn't handle non-finite values. No bound on the sum of `patch_mask` on one device may be relied on, other than what follows from the above.
Results may differ from a plain program's by a relative error of at most 0.004.
Values may be sent and summed in bfloat16 or wider, within the bound.
A program may use at most 128 MiB of HBM per device.

v0:
```python
import jax
import jax.numpy as jnp
from jax import lax
from jax.sharding import PartitionSpec as P

GROUPS = 12


eps_norm = 1e-06
clip_low = 0.8
clip_high = 1.2
spread_floor = 0.25
beta_one = 0.9
beta_two = 0.999
learn_rate = 0.001
weight_decay = 0.01
adam_eps = 1e-08
adam_count = 100.0


def modulated(latents, modulation):
    values = latents.astype(jnp.float32)
    middle = jnp.mean(values, axis=-1, keepdims=True)
    centred = values - middle
    spread = jnp.mean(centred * centred, axis=-1, keepdims=True)
    normed = centred * lax.rsqrt(spread + eps_norm)
    shift = modulation[:, 0, :][:, None, :]
    scaling = modulation[:, 1, :][:, None, :]
    return (normed * (1.0 + scaling) + shift).astype(jnp.bfloat16)


def from_groups(values):
    return lax.all_gather(values, "roll", axis=0, tiled=True)


def per_device(
    latents,
    stale_velocity,
    noise,
    modulation,
    step_ratio,
    rewards,
    group_ids,
    step_index,
    valid_steps,
    patch_mask,
    params,
    first_moment,
    second_moment,
):
    samples, patch, width = latents.shape
    rows_here = samples * patch
    contract_last = (((1,), (1,)), ((), ()))
    contract_first = (((0,), (0,)), ((), ()))
    valid = (step_index < valid_steps).astype(jnp.float32)
    member = (group_ids[:, None] == jnp.arange(GROUPS, dtype=jnp.int32)[None, :]).astype(
        jnp.float32
    )
    weighted = member * valid[:, None]
    counts, sums, squares, total_valid = lax.psum(
        (
            jnp.sum(weighted, axis=0),
            jnp.sum(weighted * rewards[:, None], axis=0),
            jnp.sum(weighted * (rewards * rewards)[:, None], axis=0),
            jnp.sum(valid),
        ),
        ("roll", "fsdp"),
    )
    hidden_in = modulated(latents, modulation).reshape(rows_here, width)
    every_rows = from_groups(hidden_in)
    weights = lax.all_gather(params.astype(jnp.bfloat16), "fsdp", axis=1, tiled=True)
    up_mat = weights[0]
    down_mat = weights[1]
    pre = jnp.dot(every_rows, up_mat, preferred_element_type=jnp.float32)
    act = jax.nn.gelu(pre).astype(jnp.bfloat16)
    branch = lax.psum_scatter(
        lax.dot_general(act, down_mat, contract_last, preferred_element_type=jnp.float32),
        "roll",
        scatter_dimension=0,
        tiled=True,
    )
    gate = 1.0 + modulation[:, 2, :]
    velocity = gate[:, None, :] * branch.reshape(samples, patch, width)
    safe = jnp.maximum(counts, 1.0)
    middle = sums / safe
    variance = jnp.maximum(squares / safe - middle * middle, 0.0)
    spread = jnp.maximum(jnp.sqrt(variance), spread_floor)
    own_mean = jnp.sum(member * middle[None, :], axis=1)
    own_spread = jnp.sum(member * spread[None, :], axis=1)
    advantage = (rewards - own_mean) / own_spread
    mask = patch_mask.astype(jnp.float32)
    npatch = jnp.maximum(jnp.sum(mask, axis=1), 1.0)
    factor = step_ratio[:, None, None]
    drawn = noise.astype(jnp.float32)
    err = drawn + factor * (stale_velocity.astype(jnp.float32) - velocity)
    logratio = jnp.sum(mask[:, :, None] * (drawn * drawn - err * err), axis=(1, 2)) / (2.0 * npatch)
    ratio = jnp.exp(logratio)
    clipped = jnp.clip(ratio, clip_low, clip_high)
    active = (ratio * advantage <= clipped * advantage).astype(jnp.float32)
    coef = -valid * advantage * ratio * active / jnp.maximum(total_valid, 1.0)
    grad_velocity = (coef / npatch)[:, None, None] * mask[:, :, None] * factor * err
    back = (gate[:, None, :] * grad_velocity).astype(jnp.bfloat16).reshape(rows_here, width)
    every_back = from_groups(back)
    grad_down = lax.dot_general(every_back, act, contract_first, preferred_element_type=jnp.float32)
    back_act = jnp.dot(every_back, down_mat, preferred_element_type=jnp.float32)
    _, pull = jax.vjp(jax.nn.gelu, pre)
    back_pre = pull(back_act)[0].astype(jnp.bfloat16)
    grad_up = lax.dot_general(
        every_rows, back_pre, contract_first, preferred_element_type=jnp.float32
    )
    grads = lax.psum_scatter(
        jnp.stack([grad_up, grad_down], axis=0), "fsdp", scatter_dimension=1, tiled=True
    )
    new_first = beta_one * first_moment + (1.0 - beta_one) * grads
    new_second = beta_two * second_moment + (1.0 - beta_two) * grads * grads
    first_hat = new_first / (1.0 - beta_one**adam_count)
    second_hat = new_second / (1.0 - beta_two**adam_count)
    update = first_hat / (jnp.sqrt(second_hat) + adam_eps) + weight_decay * params
    new_params = params - learn_rate * update
    rollout_weights = lax.all_gather(new_params.astype(jnp.bfloat16), "roll", axis=2, tiled=True)
    return (new_params, new_first, new_second, rollout_weights)


def solution(mesh):
    return jax.shard_map(
        per_device,
        mesh=mesh,
        in_specs=(
            P(("roll", "fsdp"), None, None),
            P(("roll", "fsdp"), None, None),
            P(("roll", "fsdp"), None, None),
            P(("roll", "fsdp"), None, None),
            P(("roll", "fsdp")),
            P(("roll", "fsdp")),
            P(("roll", "fsdp")),
            P(("roll", "fsdp")),
            P(("roll", "fsdp")),
            P(("roll", "fsdp"), None),
            P(None, "fsdp", "roll"),
            P(None, "fsdp", "roll"),
            P(None, "fsdp", "roll"),
        ),
        out_specs=(
            P(None, "fsdp", "roll"),
            P(None, "fsdp", "roll"),
            P(None, "fsdp", "roll"),
            P(None, "fsdp", None),
        ),
        check_vma=False,
    )
```

profile of v0, /device:TPU:1, one launch (start us, length us, event | category | flops | bytes accessed | tf_op | source)
XLA Modules:
  0.0 446.9 jit_solution(15812806068437600962)
XLA Ops:
  7.2 0.8 add_bitcast_fusion
  8.1 1.3 convert_reduce_fusion
  9.4 1.5 fusion.12
  10.9 2.7 fusion.15
  13.6 0.8 convert_element_type.40
  14.5 43.5 %all-gather.5.cloned.1.call-done = bf16[1280,2432]{1,0:T(8,128)(2,1)} async-done(((bf16[160,2432]{1,0:T(8,128)(2,1)}), bf16[1280,2432]{1,0:T(8,128)(2,1)}) %all-gather.5.cloned.1.call-update) | async-done | bytes 6225936 | tf_op jit(solution)/shard_map/all_gather | solution.py:33
  58.0 63.5 %all-gather.7.cloned.1.call-done = bf16[2,2432,640]{2,1,0:T(8,128)(2,1)} async-done(((bf16[2,152,640]{2,1,0:T(8,128)(2,1)}), bf16[2,2432,640]{2,1,0:T(8,128)(2,1)}) %all-gather.7.cloned.1.call-update) | async-done | bytes 6225936 | tf_op jit(solution)/shard_map/all_gather | solution.py:71
  121.5 8.8 %fusion.7 = f32[1280,640]{1,0:T(8,128)S(1)} fusion(bf16[1280,2432]{1,0:T(8,128)(2,1)} %all-gather.5.cloned.1.call-done, bf16[2,2432,640]{2,1,0:T(8,128)(2,1)} %all-gather.7.cloned.1.call-done), kind=kOutput, calls=%fused_computation.15 | convolution fusion | flops 3984588800 | bytes 12615680 | tf_op jit(solution)/shard_map/dot_general | solution.py:74
  130.3 1.8 copy-done.15
  132.1 8.2 %fusion.9 = f32[1280,2432]{1,0:T(8,128)} fusion(bf16[2,2432,640]{2,1,0:T(8,128)(2,1)S(1)} %copy-done.14, f32[1280,640]{1,0:T(8,128)S(1)} %fusion.7), kind=kOutput, calls=%fused_computation.17 | convolution fusion | flops 3991961600 | bytes 18841600 | tf_op jit(solution)/shard_map/dot_general | solution.py:77
  140.5 0.5 copy-done.11
  141.0 0.6 fusion.31
  141.7 66.3 %all-reduce = (f32[12]{0:T(128)S(1)}, f32[12]{0:T(128)S(1)}, f32[12]{0:T(128)S(1)}, f32[]{:T(128)}) all-reduce(f32[12]{0:T(128)S(1)} %get-tuple-element.6, f32[12]{0:T(128)S(1)} %get-tuple-element.5, f32[12]{0:T(128)S(1)} %get-tuple-element.4, f32[]{:T(128)} %get-tuple-element.19), channel_id=1, replica_groups=mesh['roll'=8,'fsdp'=16] {'roll','fsdp'}, use_global_device_ids=true, to_apply=%region_6.0 | all-reduce | flops 37 | bytes 296 | tf_op jit(solution)/shard_map/psum | solution.py:60
  209.0 3.7 reduce-scatter.3.cloned.1.call-done
  212.7 2.2 fusion.18
  215.0 1.4 multiply_convert_fusion.1
  216.6 41.2 %all-gather.9.cloned.1.call-done = bf16[1280,2432]{1,0:T(8,128)(2,1)} async-done(((bf16[160,2432]{1,0:T(8,128)(2,1)}), bf16[1280,2432]{1,0:T(8,128)(2,1)}) %all-gather.9.cloned.1.call-update) | async-done | bytes 6225936 | tf_op jit(solution)/shard_map/all_gather | solution.py:33
  257.9 22.5 %convolution_bitcast_fusion.1 = f32[1,2432,640]{2,1,0:T(8,128)} fusion(bf16[1280,2432]{1,0:T(8,128)(2,1)} %all-gather.5.cloned.1.call-done, f32[1280,640]{1,0:T(8,128)} %copy-done.15, bf16[1280,2432]{1,0:T(8,128)(2,1)} %all-gather.9.cloned.1.call-done, bf16[2,2432,640]{2,1,0:T(8,128)(2,1)} %all-gather.7.cloned.1.call-done), kind=kOutput, calls=%fused_computation.2 | convolution fusion | flops 7985561600 | bytes 25067520 | tf_op jit(solution)/shard_map/dot_general | solution.py:108
  280.4 11.9 %convolution_bitcast_fusion = f32[1,2432,640]{2,1,0:T(8,128)} fusion(bf16[1280,2432]{1,0:T(8,128)(2,1)} %all-gather.9.cloned.1.call-done, f32[1280,640]{1,0:T(8,128)} %copy-done.15), kind=kOutput, calls=%fused_computation.1 | convolution fusion | flops 3991961600 | bytes 15728640 | tf_op jit(solution)/shard_map/dot_general | solution.py:104
  292.3 8.1 %pad_maximum_fusion = f32[2,2432,640]{2,1,0:T(8,128)} fusion(f32[1,2432,640]{2,1,0:T(8,128)} %convolution_bitcast_fusion, f32[1,2432,640]{2,1,0:T(8,128)S(1)} %copy-done), kind=kLoop, calls=%fused_computation | loop fusion | flops 3112960 | bytes 24903680 | tf_op jit(solution)/shard_map/stack | solution.py:112
  300.5 103.9 %reduce-scatter.5.cloned.1.call-done = f32[2,152,640]{2,1,0:T(8,128)} async-done(((f32[2,2432,640]{2,1,0:T(8,128)}), f32[2,152,640]{2,1,0:T(8,128)}) %reduce-scatter.5.cloned.1.call-update) | async-done | bytes 778256 | tf_op jit(solution)/shard_map/reduce_scatter | solution.py:111
  404.4 3.0 fusion.29
  407.4 28.9 %all-gather.11.cloned.1.call-done = bf16[2,152,5120]{2,1,0:T(8,128)(2,1)} async-done(((bf16[2,152,640]{2,1,0:T(8,128)(2,1)}), bf16[2,152,5120]{2,1,0:T(8,128)(2,1)}) %all-gather.11.cloned.1.call-update) | async-done | bytes 3112976 | tf_op jit(solution)/shard_map/all_gather | solution.py:120
  436.3 3.7 copy.18
  (52 shorter events, 1.1 us)
Async XLA Ops:
  7.2 6.5 %copy-start.4 = (f32[2,152,640]{2,1,0:T(8,128)S(1)}, f32[2,152,640]{2,1,0:T(8,128)}, u32[]{:S(2)}) copy-start(f32[2,152,640]{2,1,0:T(8,128)} %param.23) | copy-start | bytes 2334724
  7.2 50.8 %all-gather.5.cloned.1.call-start = ((), (), s32[]{:S(2)}) async-start(), calls=%async_computation.2 | async-start | bytes 7004160 | tf_op jit(solution)/shard_map/all_gather | solution.py:33
  13.6 107.9 %all-gather.7.cloned.1.call-start = ((), (), s32[]{:S(2)}) async-start(), calls=%async_computation.3 | async-start | bytes 6615040 | tf_op jit(solution)/shard_map/all_gather | solution.py:71
  14.5 198.2 %reduce-scatter.3.cloned.1.call-start = ((), (), s32[]{:S(2)}) async-start(), calls=%async_computation.4 | async-start | bytes 14008320 | tf_op jit(solution)/shard_map/reduce_scatter | solution.py:76
  121.5 10.6 %copy-start.14 = (bf16[2,2432,640]{2,1,0:T(8,128)(2,1)S(1)}, bf16[2,2432,640]{2,1,0:T(8,128)(2,1)}, u32[]{:S(2)}) copy-start(bf16[2,2432,640]{2,1,0:T(8,128)(2,1)} %all-gather.7.cloned.1.call-done) | copy-start | bytes 18677764
  130.3 1.8 copy-start.15
  140.3 0.7 copy-start.11
  140.3 0.7 copy-start.12
  140.3 0.7 copy-start.13
  140.3 1.3 copy-start.10
  140.3 67.7 %copy-start.9 = (s32[2,80]{1,0:T(2,128)S(1)}, s32[2,80]{1,0:T(2,128)}, u32[]{:S(2)}) copy-start(s32[2,80]{1,0:T(2,128)} %param.22) | copy-start | bytes 1924
  140.4 72.3 %copy-start.2 = (bf16[2,80,2432]{2,1,0:T(8,128)(2,1)S(1)}, bf16[2,80,2432]{2,1,0:T(8,128)(2,1)}, u32[]{:S(2)}) copy-start(bf16[2,80,2432]{2,1,0:T(8,128)(2,1)} %param.14) | copy-start | bytes 2334724
  140.4 72.3 %copy-start.3 = (bf16[2,80,2432]{2,1,0:T(8,128)(2,1)S(1)}, bf16[2,80,2432]{2,1,0:T(8,128)(2,1)}, u32[]{:S(2)}) copy-start(bf16[2,80,2432]{2,1,0:T(8,128)(2,1)} %param.15) | copy-start | bytes 2334724
  140.4 72.3 %copy-start.8 = (f32[2]{0:T(128)S(1)}, f32[2]{0:T(128)}, u32[]{:S(2)}) copy-start(f32[2]{0:T(128)} %param.17) | copy-start | bytes 28
  140.4 117.4 %all-gather.9.cloned.1.call-start = ((), (), s32[]{:S(2)}) async-start(), calls=%async_computation.5 | async-start | bytes 7004160 | tf_op jit(solution)/shard_map/all_gather | solution.py:33
  212.6 2.3 copy-start.1
  216.4 187.9 %reduce-scatter.5.cloned.1.call-start = ((), (), s32[]{:S(2)}) async-start(), calls=%async_computation.6 | async-start | bytes 13230080 | tf_op jit(solution)/shard_map/reduce_scatter | solution.py:111
  280.4 11.9 %copy-start = (f32[1,2432,640]{2,1,0:T(8,128)S(1)}, f32[1,2432,640]{2,1,0:T(8,128)}, u32[]{:S(2)}) copy-start(f32[1,2432,640]{2,1,0:T(8,128)} %convolution_bitcast_fusion.1) | copy-start | bytes 18677764
  300.4 104.0 %copy-start.5 = (f32[2,152,640]{2,1,0:T(8,128)S(1)}, f32[2,152,640]{2,1,0:T(8,128)}, u32[]{:S(2)}) copy-start(f32[2,152,640]{2,1,0:T(8,128)} %param.23) | copy-start | bytes 2334724
  300.4 104.0 %copy-start.6 = (f32[2,152,640]{2,1,0:T(8,128)S(1)}, f32[2,152,640]{2,1,0:T(8,128)}, u32[]{:S(2)}) copy-start(f32[2,152,640]{2,1,0:T(8,128)} %param.24) | copy-start | bytes 2334724
  300.4 104.0 %copy-start.7 = (f32[2,152,640]{2,1,0:T(8,128)S(1)}, f32[2,152,640]{2,1,0:T(8,128)}, u32[]{:S(2)}) copy-start(f32[2,152,640]{2,1,0:T(8,128)} %param.25) | copy-start | bytes 2334724
  300.4 135.9 %all-gather.11.cloned.1.call-start = ((), (), s32[]{:S(2)}) async-start(), calls=%async_computation.7 | async-start | bytes 3502080 | tf_op jit(solution)/shard_map/all_gather | solution.py:120
Sparse Core Ops, SparseCore 0:
  13.7 44.2 all-gather.4
  60.8 60.6 all-gather.6
  140.5 72.0 reduce-scatter.2
  216.5 41.2 all-gather.8
  300.5 103.7 reduce-scatter.4
  407.5 28.7 all-gather.10
where the time goes:
time: 447 us
  waiting for transfers between devices  285 us (64%)
  blocking collectives  66.3 us (15%)
  matrix products  51.4 us (11%)
  other arithmetic  23 us (5%)
  between operations  14.9 us (3%)
  local copies, waits for them, and re-layouts  6.15 us (1%)
    reduce_scatter x1, waiting for transfers between devices, per_device(): lax.psum_scatter(jnp.stack([grad_up, grad_down], axis=0), 'fsdp', scatter...  104 us
    all_gather x2, waiting for transfers between devices, from_groups(): return lax.all_gather(values, 'roll', axis=0, tiled=True)  84.7 us
    psum x1, blocking collectives, per_device(): lax.psum((jnp.sum(weighted, axis=0), jnp.sum(weighted * rewards[:, None],...  66.3 us
    all_gather x1, waiting for transfers between devices, per_device(): lax.all_gather(params.astype(jnp.bfloat16), 'fsdp', axis=1, tiled=True)  63.5 us
    all_gather x1, waiting for transfers between devices, per_device(): lax.all_gather(new_params.astype(jnp.bfloat16), 'roll', axis=2, tiled=True)  28.9 us
    dot_general x1, matrix products, per_device(): lax.dot_general(every_rows, back_pre, contract_first, preferred_element_t...  22.5 us
    dot_general x1, matrix products, per_device(): lax.dot_general(every_back, act, contract_first, preferred_element_type=j...  11.9 us
  transfers between devices with their start and end apart: 6, of which 6 were waited for; matrix products, arithmetic and copies ran while one was open for 0% of the time, Pallas kernels for 0%

commit v1 on v0

v1 whole, which is shorter than its diff:
```python
import functools

import jax
import jax.numpy as jnp
from jax import lax
from jax.experimental import pallas as pl
from jax.experimental.pallas import tpu as pltpu
from jax.sharding import PartitionSpec as P

GROUPS = 12
D = 2432
BLOCK = 152
SLICE = 640
PATCH = 80
CHUNK = 16

eps_norm = 1e-06
clip_low = 0.8
clip_high = 1.2
spread_floor = 0.25
beta_one = 0.9
beta_two = 0.999
learn_rate = 0.001
weight_decay = 0.01
adam_eps = 1e-08
adam_count = 100.0

BF = jnp.bfloat16
F32 = jnp.float32
MESH = pl.DeviceIdType.MESH
TILES = ((0, 640), (640, 640), (1280, 640), (1920, 512))
COLS = (pl.ds(0, 1280), pl.ds(1280, 1152))
OUT_COLS = ((0, 384), (384, 256))
LAST = (((1,), (1,)), ((), ()))
FIRST = (((0,), (0,)), ((), ()))
N_COPIES = 180


def gelu_parts(pre):
    root = 0.7978845608028654
    square = pre * pre
    t = jnp.tanh(root * (pre + 0.044715 * (square * pre)))
    cdf = 0.5 * (1.0 + t)
    slope = cdf + pre * (0.5 * (1.0 - t * t)) * (root * (1.0 + (3.0 * 0.044715) * square))
    return pre * cdf, slope


def kernel(
    rewards,
    group_ids,
    step_index,
    valid_steps,
    step_ratio,
    mask_in,
    mod,
    lat_h,
    stale_h,
    noise_h,
    par_h,
    m1_h,
    m2_h,
    o_par,
    o_m1,
    o_m2,
    o_roll,
    hid,
    bk,
    raw0,
    raw1,
    asm_up,
    asm_down,
    pre,
    act,
    sib_recv,
    y_send,
    y_recv,
    own,
    grad,
    x_recv,
    grad_own,
    b_send,
    b_recv,
    lat,
    stale,
    noise,
    par,
    m1,
    m2,
    fresh,
    mask_col,
    stats,
    stats_recv,
    send_sem,
    recv_sem,
    local_sem,
):
    roll = lax.axis_index("roll")
    fsdp = lax.axis_index("fsdp")
    y, c = roll // 2, lax.rem(roll, 2)
    x, z = fsdp // 4, lax.rem(fsdp, 4)

    def turn(a, by):
        return lax.rem(a + by, 4)

    def at(x_, y_, z_, c_):
        return (y_ * 2 + c_, x_ * 4 + z_)

    y_ring = [at(x, turn(y, j), z, c) for j in range(4)]
    x_ring = [at(turn(x, j), y, z, c) for j in range(4)]
    z_ring = [at(x, y, turn(z, j), c) for j in range(4)]
    sibling = at(x, y, z, 1 - c)
    y_plus, y_minus = y_ring[1], y_ring[3]

    barrier = pltpu.get_barrier_semaphore()
    partners = y_ring[1:] + x_ring[1:] + z_ring[1:] + [sibling]
    for partner in partners:
        pl.semaphore_signal(barrier, inc=1, device_id=partner, device_id_type=MESH)

    count = [0]
    sent = []

    def push(src, dst, device, landed=None, keep=True):
        i = count[0]
        count[0] += 1
        copy = pltpu.make_async_remote_copy(
            src_ref=src,
            dst_ref=dst,
            send_sem=send_sem.at[i],
            recv_sem=recv_sem.at[i],
            device_id=device,
            device_id_type=MESH,
        )
        copy.start()
        if keep:
            sent.append(copy)
        if landed is None:
            return copy
        return pltpu.make_async_remote_copy(
            src_ref=landed,
            dst_ref=landed,
            send_sem=send_sem.at[i],
            recv_sem=recv_sem.at[i],
            device_id=device,
            device_id_type=MESH,
        )

    local = [0]

    def move(src, dst):
        i = local[0]
        local[0] += 1
        copy = pltpu.make_async_copy(src, dst, local_sem.at[i])
        copy.start()
        return copy

    par_in = move(par_h, par)
    lat_in = move(lat_h, lat)
    stale_in = move(stale_h, stale)
    noise_in = move(noise_h, noise)
    m1_in = move(m1_h, m1)
    m2_in = move(m2_h, m2)

    raws = (raw0, raw1)
    near = (x_ring, z_ring)
    far = (z_ring, x_ring)
    near_at = (x, z)
    far_at = (z, x)

    par_in.wait()
    for m in range(2):
        raw0[m, z, x] = par[m, 0:80, :].astype(BF)
        raw1[m, x, z, 0:72, :] = par[m, 80:BLOCK, :].astype(BF)
        raw1[m, x, z, 64:80, :] = jnp.concatenate(
            [par[m, 144:BLOCK, :], jnp.zeros((8, SLICE), F32)], axis=0
        ).astype(BF)

    def modulated(s):
        shift = mod[0, s : s + 1, :]
        scaling = 1.0 + mod[1, s : s + 1, :]

        def body(i, carry):
            rows = pl.ds(pl.multiple_of(i * CHUNK, CHUNK), CHUNK)
            values = lat[s, rows, :].astype(F32)
            middle = jnp.sum(values, axis=-1, keepdims=True) / D
            centred = values - middle
            spread = jnp.sum(centred * centred, axis=-1, keepdims=True) / D
            normed = centred * lax.rsqrt(spread + eps_norm)
            hid[s, 0, 0, rows, :] = (normed * scaling + shift).astype(BF)
            return carry

        lax.fori_loop(0, PATCH // CHUNK, body, 0)

    pl.semaphore_wait(barrier, len(partners))

    first = {}
    for m in range(2):
        for h in range(2):
            a, b = far_at[h], near_at[h]
            mine = raws[h].at[m, a, b]
            first[m, h, 0] = push(mine, mine, near[h][1], raws[h].at[m, a, turn(b, 3)])
            first[m, h, 1] = push(mine, mine, near[h][3], raws[h].at[m, a, turn(b, 1)])

    lat_in.wait()

    def gather_own(buf, s):
        mine = buf.at[s, 0, 0]
        left, right = buf.at[s, 0, 3], buf.at[s, 0, 1]
        lo, hi = COLS
        return {
            "left_lo": push(mine.at[:, lo], left.at[:, lo], y_plus),
            "right_hi": push(mine.at[:, hi], right.at[:, hi], y_minus),
            "left_hi": push(mine.at[:, hi], left.at[:, hi], y_plus),
            "right_lo": push(mine.at[:, lo], right.at[:, lo], y_minus),
            "sib0": push(mine, buf.at[s, 1, 0], sibling),
        }

    def gather_on(buf, s, d):
        left, right, across = buf.at[s, 0, 3], buf.at[s, 0, 1], buf.at[s, 0, 2]
        lo, hi = COLS
        d["left_lo"].wait_recv()
        d["across_lo"] = push(left.at[:, lo], across.at[:, lo], y_plus)
        d["right_hi"].wait_recv()
        d["across_hi"] = push(right.at[:, hi], across.at[:, hi], y_minus)

    def gather_near(buf, s, d):
        d["left_hi"].wait_recv()
        d["sib3"] = push(buf.at[s, 0, 3], buf.at[s, 1, 3], sibling)
        d["right_lo"].wait_recv()
        d["sib1"] = push(buf.at[s, 0, 1], buf.at[s, 1, 1], sibling)

    def gather_end(buf, s, d):
        d["across_lo"].wait_recv()
        d["across_hi"].wait_recv()
        d["sib2"] = push(buf.at[s, 0, 2], buf.at[s, 1, 2], sibling)

    def gather_sib(d):
        for j in range(4):
            d["sib%d" % j].wait_recv()

    modulated(0)
    rows0 = gather_own(hid, 0)
    modulated(1)

    lane = lax.broadcasted_iota(jnp.int32, (1, 128), 1)
    valid = [jnp.where(step_index[s] < valid_steps[s], 1.0, 0.0).astype(F32) for s in range(2)]
    member = [jnp.where(lane == group_ids[s], 1.0, 0.0).astype(F32) for s in range(2)]
    stats[...] = jnp.zeros((8, 128), F32)
    stats[0:1, :] = member[0] * valid[0] + member[1] * valid[1]
    stats[1:2, :] = member[0] * (valid[0] * rewards[0]) + member[1] * (valid[1] * rewards[1])
    stats[2:3, :] = member[0] * (valid[0] * (rewards[0] * rewards[0])) + member[1] * (
        valid[1] * (rewards[1] * rewards[1])
    )
    stats[3:4, :] = jnp.zeros((1, 128), F32) + (valid[0] + valid[1])

    def stats_send(step):
        ring = ([None, sibling], y_ring, x_ring, z_ring)[step]
        copies = []
        for j in range(1, len(ring)):
            slot = stats_recv.at[step, j]
            copies.append(push(stats, slot, ring[j], keep=False))
        return copies

    def stats_sum(step, copies):
        total = stats[...]
        for j, copy in enumerate(copies):
            copy.wait_recv()
            total = total + stats_recv[step, j + 1]
        for copy in copies:
            copy.wait_send()
        stats[...] = total

    stats_copies = stats_send(0)

    def pass_on(m):
        for h in range(2):
            a, b = far_at[h], near_at[h]
            got = (turn(b, 3), turn(b, 1))[m]
            step = (1, 3)[m]
            first[m, h, m].wait_recv()
            block = raws[h].at[m, a, got]
            first[m, h, 2] = push(block, block, near[h][step], raws[h].at[m, a, turn(b, 2)])

    second = {}

    def groups(m):
        for h in range(2):
            first[m, h, 1 - m].wait_recv()
            first[m, h, 2].wait_recv()
            a = far_at[h]
            lo, hi = (raws[h].at[m, a, pl.ds(k, 2)] for k in (0, 2))
            left, right = turn(a, 3), turn(a, 1)
            second[m, h, "left_lo"] = push(lo, lo, far[h][1], raws[h].at[m, left, pl.ds(0, 2)])
            second[m, h, "right_hi"] = push(hi, hi, far[h][3], raws[h].at[m, right, pl.ds(2, 2)])
            second[m, h, "left_hi"] = push(hi, hi, far[h][1], raws[h].at[m, left, pl.ds(2, 2)])
            second[m, h, "right_lo"] = push(lo, lo, far[h][3], raws[h].at[m, right, pl.ds(0, 2)])

    def groups_on(m):
        for h in range(2):
            a = far_at[h]
            left, right, across = turn(a, 3), turn(a, 1), turn(a, 2)
            second[m, h, "left_lo"].wait_recv()
            block = raws[h].at[m, left, pl.ds(0, 2)]
            second[m, h, "across_lo"] = push(
                block, block, far[h][1], raws[h].at[m, across, pl.ds(0, 2)]
            )
            second[m, h, "right_hi"].wait_recv()
            block = raws[h].at[m, right, pl.ds(2, 2)]
            second[m, h, "across_hi"] = push(
                block, block, far[h][3], raws[h].at[m, across, pl.ds(2, 2)]
            )

    def assemble(m, out):
        for h in range(2):
            for part in ("left_hi", "right_lo", "across_lo", "across_hi"):
                second[m, h, part].wait_recv()

        def body(i, carry):
            base = pl.multiple_of(i * (4 * BLOCK), CHUNK)
            parts = []
            for k in range(4):
                parts += [raw0[m, k, i], raw1[m, i, k, 0:72, :]]
            out[pl.ds(base, 4 * BLOCK), :] = jnp.concatenate(parts, axis=0)
            return carry

        lax.fori_loop(0, 4, body, 0)

    pass_on(0)
    pass_on(1)
    gather_on(hid, 0, rows0)
    groups(0)
    rows1 = gather_own(hid, 1)
    stats_sum(0, stats_copies)
    stats_copies = stats_send(1)
    gather_near(hid, 0, rows0)
    groups_on(0)
    groups(1)
    stats_sum(1, stats_copies)
    stats_copies = stats_send(2)
    gather_end(hid, 0, rows0)
    gather_on(hid, 1, rows1)
    stats_sum(2, stats_copies)
    stats_copies = stats_send(3)

    diag = lax.broadcasted_iota(jnp.int32, (PATCH, PATCH), 0) == lax.broadcasted_iota(
        jnp.int32, (PATCH, PATCH), 1
    )
    npatch = []
    for s in range(2):
        row = jnp.broadcast_to(mask_in[s : s + 1, :].astype(F32), (PATCH, PATCH))
        column = jnp.sum(jnp.where(diag, row, 0.0), axis=1, keepdims=True)
        mask_col[s] = jnp.broadcast_to(column, (PATCH, 128))
        npatch.append(jnp.maximum(jnp.sum(column, axis=0, keepdims=True), 1.0))

    stats_sum(3, stats_copies)

    def forward(s):
        def body(i, carry):
            rows = hid[s, i].reshape(4 * PATCH, D)
            value = jnp.dot(rows, asm_up[0:D, :], preferred_element_type=F32)
            pre[s, i] = value
            act[s, i] = gelu_parts(value)[0].astype(BF)
            return carry

        lax.fori_loop(0, 2, body, 0)

    assemble(0, asm_up)
    gather_sib(rows0)
    forward(0)
    gather_near(hid, 1, rows1)
    groups_on(1)
    gather_end(hid, 1, rows1)
    gather_sib(rows1)
    forward(1)
    assemble(1, asm_down)

    def branch_tile(s, i, n):
        start, width = TILES[n]
        return lax.dot_general(
            act[s, i], asm_down[start : start + width, :], LAST, preferred_element_type=F32
        )

    pair = {}

    def branch_away(s):
        for n, (start, width) in enumerate(TILES):
            slot = asm_up.at[pl.ds((s * 4 + n) * 320, 320)]
            slot[:, 0:width] = branch_tile(s, 1, n).astype(BF)
            pair[s, n] = push(slot, sib_recv.at[s, n], sibling)

    def branch_mine(s):
        for n, (start, width) in enumerate(TILES):
            value = branch_tile(s, 0, n)
            pair[s, n].wait_recv()
            value = value + sib_recv[s, n, :, 0:width].astype(F32)
            cols = slice(start, start + width)
            own[s, :, cols] = value[0:80]
            for j, k in ((2, 0), (1, 1), (3, 2)):
                y_send[s, k, :, cols] = value[j * 80 : j * 80 + 80].astype(BF)

    def ring_start(send, recv, parts, plus, minus):
        lo, hi = parts
        return {
            "across_hi": push(hi(send, 0), hi(recv, 0), plus),
            "across_lo": push(lo(send, 0), lo(recv, 0), minus),
            "plus_lo": push(lo(send, 1), lo(recv, 1), plus),
            "minus_hi": push(hi(send, 2), hi(recv, 2), minus),
        }

    def ring_add(send, recv, parts, plus, minus, add, d):
        lo, hi = parts
        d["across_hi"].wait_recv()
        add(hi(send, 1), hi(recv, 0))
        d["plus_hi"] = push(hi(send, 1), hi(recv, 1), plus)
        d["across_lo"].wait_recv()
        add(lo(send, 2), lo(recv, 0))
        d["minus_lo"] = push(lo(send, 2), lo(recv, 2), minus)

    def ring_wait(d):
        for part in ("plus_lo", "minus_hi", "plus_hi", "minus_lo"):
            d[part].wait_recv()

    def add_rows(dst, src):
        def body(i, carry):
            rows = pl.ds(pl.multiple_of(i * CHUNK, CHUNK), CHUNK)
            dst[rows, :] = (dst[rows, :].astype(F32) + src[rows, :].astype(F32)).astype(BF)
            return carry

        lax.fori_loop(0, dst.shape[0] // CHUNK, body, 0)

    def add_blocks(dst, src):
        for k in range(2):
            dst[k] = (dst[k].astype(F32) + src[k].astype(F32)).astype(BF)

    col_parts = tuple((lambda ref, k, cols=cols: ref.at[k, :, cols]) for cols in COLS)
    block_parts = tuple((lambda ref, k, i=i: ref.at[k, pl.ds(i, 2)]) for i in (0, 2))
    row_parts = tuple((lambda ref, k, r=r: ref.at[k, pl.ds(*r)]) for r in ((0, 48), (48, 32)))

    def branch_ring(s):
        return ring_start(y_send.at[s], y_recv.at[s], col_parts, y_plus, y_minus)

    def branch_add(s, d):
        ring_add(y_send.at[s], y_recv.at[s], col_parts, y_plus, y_minus, add_rows, d)

    def back_rows(s, d):
        ring_wait(d)
        gate = 1.0 + mod[2, s : s + 1, :]
        factor = step_ratio[s]

        def err_body(i, total):
            rows = pl.ds(pl.multiple_of(i * CHUNK, CHUNK), CHUNK)
            branch = (
                own[s, rows, :] + y_recv[s, 1, rows, :].astype(F32) + y_recv[s, 2, rows, :].astype(F32)
            )
            velocity = gate * branch
            drawn = noise[s, rows, :].astype(F32)
            err = drawn + factor * (stale[s, rows, :].astype(F32) - velocity)
            own[s, rows, :] = err
            gap = jnp.sum(drawn * drawn - err * err, axis=1, keepdims=True)
            return total + mask_col[s, rows, 0:1] * gap

        gaps = lax.fori_loop(0, PATCH // CHUNK, err_body, jnp.zeros((CHUNK, 1), F32))
        logratio = jnp.sum(gaps, axis=0, keepdims=True) / (2.0 * npatch[s])
        safe = jnp.maximum(stats[0:1, :], 1.0)
        middle = stats[1:2, :] / safe
        variance = jnp.maximum(stats[2:3, :] / safe - middle * middle, 0.0)
        spread = jnp.maximum(jnp.sqrt(variance), spread_floor)
        own_mean = jnp.sum(member[s] * middle, axis=1, keepdims=True)
        own_spread = jnp.sum(member[s] * spread, axis=1, keepdims=True)
        advantage = (rewards[s] - own_mean) / own_spread
        ratio = jnp.exp(logratio)
        clipped = jnp.clip(ratio, clip_low, clip_high)
        active = jnp.where(ratio * advantage <= clipped * advantage, 1.0, 0.0).astype(F32)
        coef = -valid[s] * advantage * ratio * active / jnp.maximum(stats[3:4, 0:1], 1.0)
        per_patch = coef / npatch[s]

        def back_body(i, carry):
            rows = pl.ds(pl.multiple_of(i * CHUNK, CHUNK), CHUNK)
            scale = per_patch * mask_col[s, rows, 0:1] * factor
            bk[s, 0, 0, rows, :] = (gate * (scale * own[s, rows, :])).astype(BF)
            return carry

        lax.fori_loop(0, PATCH // CHUNK, back_body, 0)

    branch_away(0)
    branch_mine(0)
    ring0 = branch_ring(0)
    branch_away(1)
    branch_mine(1)
    branch_add(0, ring0)
    ring1 = branch_ring(1)
    stale_in.wait()
    noise_in.wait()
    back_rows(0, ring0)
    branch_add(1, ring1)
    back0 = gather_own(bk, 0)
    back_rows(1, ring1)
    gather_on(bk, 0, back0)
    back1 = gather_own(bk, 1)
    gather_near(bk, 0, back0)
    gather_end(bk, 0, back0)
    gather_sib(back0)

    def back_pre(s):
        def body(i, carry):
            rows = bk[s, i].reshape(4 * PATCH, D)
            value = jnp.dot(rows, asm_down[...], preferred_element_type=F32)
            act[s, i] = (value * gelu_parts(pre[s, i])[1]).astype(BF)
            return carry

        lax.fori_loop(0, 2, body, 0)

    def grad_tile(rows, s, n):
        start, width = TILES[n]
        left = rows[s, :, :, :, start : start + width].reshape(8 * PATCH, width)
        right = act[s].reshape(8 * PATCH, SLICE)
        return lax.dot_general(left, right, FIRST, preferred_element_type=F32)

    def grad_rows(h, j, k):
        a, b = turn(far_at[h], j), turn(near_at[h], k)
        block = (b * 4 + a) if h == 0 else (a * 4 + b)
        return grad[pl.ds(pl.multiple_of(block * BLOCK + 80 * h, 8), 80), :]

    def far_start(m):
        for j, slot in ((2, 0), (1, 1), (3, 2)):
            for h in range(2):
                for k in range(4):
                    raws[h][m, slot, k] = grad_rows(h, j, k).astype(BF)
        out = [
            ring_start(raws[h].at[m], x_recv.at[m, h], block_parts, far[h][1], far[h][3])
            for h in range(2)
        ]
        for h in range(2):
            for k in range(4):
                grad_own[m, h, k] = grad_rows(h, 0, k)
        return out

    def far_add(m, d):
        for h in range(2):
            ring_add(
                raws[h].at[m],
                x_recv.at[m, h],
                block_parts,
                far[h][1],
                far[h][3],
                add_blocks,
                d[h],
            )

    def near_start(m, d):
        out = []
        for h in range(2):
            ring_wait(d[h])
            for k in (2, 1, 3, 0):
                total = (
                    grad_own[m, h, k] + x_recv[m, h, 1, k].astype(F32) + x_recv[m, h, 2, k].astype(F32)
                )
                if k == 0:
                    grad_own[m, h, 0] = total
                else:
                    b_send[m, h, {2: 0, 1: 1, 3: 2}[k]] = total.astype(BF)
            out.append(
                ring_start(b_send.at[m, h], b_recv.at[m, h], row_parts, near[h][1], near[h][3])
            )
        return out

    def near_add(m, d):
        for h in range(2):
            ring_add(
                b_send.at[m, h],
                b_recv.at[m, h],
                row_parts,
                near[h][1],
                near[h][3],
                add_rows,
                d[h],
            )

    def out_cols(owner, start, width):
        return pl.ds(pl.multiple_of(owner * SLICE + start, 128), width)

    out_copies = []

    def update(m, d):
        for h in range(2):
            ring_wait(d[h])
            rows = slice(0, 80) if h == 0 else slice(80, BLOCK)
            high = 80 if h == 0 else 72
            grads = (
                grad_own[m, h, 0, 0:high, :]
                + b_recv[m, h, 1, 0:high, :].astype(F32)
                + b_recv[m, h, 2, 0:high, :].astype(F32)
            )
            weights = par[m, rows, :]
            new_first = beta_one * m1[m, rows, :] + (1.0 - beta_one) * grads
            new_second = beta_two * m2[m, rows, :] + (1.0 - beta_two) * grads * grads
            first_hat = new_first / (1.0 - beta_one**adam_count)
            second_hat = new_second / (1.0 - beta_two**adam_count)
            step = first_hat / (jnp.sqrt(second_hat) + adam_eps) + weight_decay * weights
            new_weights = weights - learn_rate * step
            m1[m, rows, :] = new_first
            m2[m, rows, :] = new_second
            par[m, rows, :] = new_weights
            fresh[m, rows, :] = new_weights.astype(BF)
        d = {}
        place = o_roll.at[m, :, out_cols(roll, 0, SLICE)]
        left = o_roll.at[m, :, out_cols(turn(y, 3) * 2 + c, 0, SLICE)]
        right = o_roll.at[m, :, out_cols(turn(y, 1) * 2 + c, 0, SLICE)]
        d["left"] = push(fresh.at[m], place, y_plus, left)
        d["right"] = push(fresh.at[m], place, y_minus, right)
        other = o_roll.at[m, :, out_cols(y * 2 + 1 - c, 0, SLICE)]
        d["sib0"] = push(fresh.at[m], place, sibling, other)
        out_copies.append(move(fresh.at[m], place))
        out_copies.append(move(m1.at[m], o_m1.at[m]))
        out_copies.append(move(m2.at[m], o_m2.at[m]))
        out_copies.append(move(par.at[m], o_par.at[m]))
        return d

    def out_on(m, d):
        across = turn(y, 2)
        for key, by, to, half in (("left", 3, y_plus, 0), ("right", 1, y_minus, 1)):
            owner = turn(y, by)
            d[key].wait_recv()
            start, width = OUT_COLS[half]
            block = o_roll.at[m, :, out_cols(owner * 2 + c, start, width)]
            landed = o_roll.at[m, :, out_cols(across * 2 + c, start, width)]
            d[key, "across"] = push(block, block, to, landed)
            whole = o_roll.at[m, :, out_cols(owner * 2 + c, 0, SLICE)]
            twin = o_roll.at[m, :, out_cols(owner * 2 + 1 - c, 0, SLICE)]
            d[key, "sib"] = push(whole, whole, sibling, twin)

    def out_end(m, d):
        across = turn(y, 2)
        d["left", "across"].wait_recv()
        d["right", "across"].wait_recv()
        whole = o_roll.at[m, :, out_cols(across * 2 + c, 0, SLICE)]
        twin = o_roll.at[m, :, out_cols(across * 2 + 1 - c, 0, SLICE)]
        d["sib2"] = push(whole, whole, sibling, twin)

    def out_sib(d):
        d["sib0"].wait_recv()
        d["left", "sib"].wait_recv()
        d["right", "sib"].wait_recv()
        d["sib2"].wait_recv()

    for copy in sent:
        copy.wait_send()
    sent.clear()
    grad[pl.ds(D, 8), :] = jnp.zeros((8, SLICE), F32)

    for n, (start, width) in enumerate(TILES):
        grad[start : start + width, :] = grad_tile(bk, 0, n)
    gather_on(bk, 1, back1)
    back_pre(0)
    gather_near(bk, 1, back1)
    gather_end(bk, 1, back1)
    gather_sib(back1)
    for n, (start, width) in enumerate(TILES):
        grad[start : start + width, :] += grad_tile(bk, 1, n)
    down_far = far_start(1)
    back_pre(1)
    far_add(1, down_far)
    for n, (start, width) in enumerate(TILES):
        grad[start : start + width, :] = grad_tile(hid, 0, n) + grad_tile(hid, 1, n)
    up_far = far_start(0)
    m1_in.wait()
    m2_in.wait()
    down_near = near_start(1, down_far)
    far_add(0, up_far)
    near_add(1, down_near)
    down_out = update(1, down_near)
    out_on(1, down_out)
    up_near = near_start(0, up_far)
    near_add(0, up_near)
    out_end(1, down_out)
    up_out = update(0, up_near)
    out_on(0, up_out)
    out_sib(down_out)
    out_end(0, up_out)
    out_sib(up_out)
    for copy in out_copies:
        copy.wait()
    for copy in sent:
        copy.wait_send()


def per_device(
    latents,
    stale_velocity,
    noise,
    modulation,
    step_ratio,
    rewards,
    group_ids,
    step_index,
    valid_steps,
    patch_mask,
    params,
    first_moment,
    second_moment,
):
    any_ = pl.BlockSpec(memory_space=pl.ANY)
    smem = pl.BlockSpec(memory_space=pltpu.SMEM)
    vmem = pl.BlockSpec(memory_space=pltpu.VMEM)
    shard = jax.ShapeDtypeStruct(params.shape, F32)
    outs = pl.pallas_call(
        kernel,
        out_shape=(shard, shard, shard, jax.ShapeDtypeStruct((2, BLOCK, 8 * SLICE), BF)),
        in_specs=[smem] * 5 + [vmem] * 2 + [any_] * 6,
        out_specs=(any_,) * 4,
        scratch_shapes=[
            pltpu.VMEM((2, 2, 4, PATCH, D), BF),
            pltpu.VMEM((2, 2, 4, PATCH, D), BF),
            pltpu.VMEM((2, 4, 4, 80, SLICE), BF),
            pltpu.VMEM((2, 4, 4, 80, SLICE), BF),
            pltpu.VMEM((2560, SLICE), BF),
            pltpu.VMEM((D, SLICE), BF),
            pltpu.VMEM((2, 2, 4 * PATCH, SLICE), F32),
            pltpu.VMEM((2, 2, 4 * PATCH, SLICE), BF),
            pltpu.VMEM((2, 4, 4 * PATCH, SLICE), BF),
            pltpu.VMEM((2, 3, PATCH, D), BF),
            pltpu.VMEM((2, 3, PATCH, D), BF),
            pltpu.VMEM((2, PATCH, D), F32),
            pltpu.VMEM((D + 8, SLICE), F32),
            pltpu.VMEM((2, 2, 3, 4, 80, SLICE), BF),
            pltpu.VMEM((2, 2, 4, 80, SLICE), F32),
            pltpu.VMEM((2, 2, 3, 80, SLICE), BF),
            pltpu.VMEM((2, 2, 3, 80, SLICE), BF),
            pltpu.VMEM((2, PATCH, D), BF),
            pltpu.VMEM((2, PATCH, D), BF),
            pltpu.VMEM((2, PATCH, D), BF),
            pltpu.VMEM((2, BLOCK, SLICE), F32),
            pltpu.VMEM((2, BLOCK, SLICE), F32),
            pltpu.VMEM((2, BLOCK, SLICE), F32),
            pltpu.VMEM((2, BLOCK, SLICE), BF),
            pltpu.VMEM((2, PATCH, 128), F32),
            pltpu.VMEM((8, 128), F32),
            pltpu.VMEM((4, 4, 8, 128), F32),
            pltpu.SemaphoreType.DMA((N_COPIES,)),
            pltpu.SemaphoreType.DMA((N_COPIES,)),
            pltpu.SemaphoreType.DMA((16,)),
        ],
        compiler_params=pltpu.CompilerParams(
            collective_id=0, has_side_effects=True, vmem_limit_bytes=63 << 20
        ),
    )(
        rewards,
        group_ids,
        step_index,
        valid_steps,
        step_ratio,
        patch_mask,
        modulation.transpose(1, 0, 2),
        latents,
        stale_velocity,
        noise,
        params,
        first_moment,
        second_moment,
    )
    return tuple(outs)


def solution(mesh):
    rows = ("roll", "fsdp")
    weights = P(None, "fsdp", "roll")
    return jax.shard_map(
        per_device,
        mesh=mesh,
        in_specs=(
            P(rows, None, None),
            P(rows, None, None),
            P(rows, None, None),
            P(rows, None, None),
            P(rows),
            P(rows),
            P(rows),
            P(rows),
            P(rows),
            P(rows, None),
            weights,
            weights,
            weights,
        ),
        out_specs=(weights, weights, weights, P(None, "fsdp", None)),
        check_vma=False,
    )
```

time: 447 us -> 190 us (0.43)
  waiting for transfers between devices: 285 us -> 0 us
  Pallas kernels: 0 us -> 180 us
  blocking collectives: 66.3 us -> 0 us
  matrix products: 51.4 us -> 0 us
  other arithmetic: 23 us -> 0 us
  between operations: 14.9 us -> 0.65 us
    pallas_call x0 -> x1, Pallas kernels: none -> 180 us  [per_device(): pl.pallas_call(kernel, out_shape=(shard, shard, shard, jax.ShapeDtypeStru...]
    all_gather x4 -> x0, waiting for transfers between devices: 177 us -> none  [the longest x2 84.7 us: from_groups(): return lax.all_gather(values, 'roll', axis=0, tiled=True)]
    reduce_scatter x2 -> x0, waiting for transfers between devices: 108 us -> none  [the longest x1 104 us: per_device(): lax.psum_scatter(jnp.stack([grad_up, grad_down], axis=0), 'fsdp', scatter...]
    psum x1 -> x0, blocking collectives: 66.3 us -> none  [per_device(): lax.psum((jnp.sum(weighted, axis=0), jnp.sum(weighted * rewards[:, None],...]
    dot_general x4 -> x0, matrix products: 51.4 us -> none  [the longest x1 22.5 us: per_device(): lax.dot_general(every_rows, back_pre, contract_first, preferred_element_t...]
    another operation x1 -> x0, other arithmetic: 8.09 us -> none  [per_device(): jnp.stack([grad_up, grad_down], axis=0)]
    convert_element_type x5 -> x0, other arithmetic: 7.87 us -> none  [the longest x1 3.03 us: per_device(): new_params.astype(jnp.bfloat16)]
    reduce_sum x7 -> x0, other arithmetic: 6.05 us -> none  [the longest x1 2.23 us: per_device(): jnp.sum(mask[:, :, None] * (drawn * drawn - err * err), axis=(1, 2))]
  transfers between devices with their start and end apart: 6 -> 0, of which waited for: 6 -> 0; matrix products, arithmetic and copies ran while one was open for 0% -> 0% of each run, Pallas kernels for 0% -> 0%
where the time goes in v1:
time: 190 us; the launch traced here: 189 us
  Pallas kernels  180 us (95%)
  local copies, waits for them, and re-layouts  7.98 us (4%)
    pallas_call x1, Pallas kernels, per_device(): pl.pallas_call(kernel, out_shape=(shard, shard, shard, jax.ShapeDtypeStru...  180 us
    unnamed x6, local copies, waits for them, and re-layouts  7.98 us

profile of v1, /device:TPU:1, one launch (start us, length us, event | category | flops | bytes accessed | tf_op | source)
XLA Modules:
  0.0 188.7 jit_solution(11514027314675374773)
XLA Ops:
  0.6 180.1 %shard_map.156 = (f32[2,152,640]{2,1,0:T(8,128)}, f32[2,152,640]{2,1,0:T(8,128)}, f32[2,152,640]{2,1,0:T(8,128)}, bf16[2,152,5120]{2,1,0:T(8,128)(2,1)}) custom-call(f32[2]{0:T(128)} %rewards.1, s32[2]{0:T(128)} %group_ids.1, s32[2]{0:T(128)} %step_index.1, s32[2]{0:T(128)} %valid_steps.1, f32[2]{0:T(128)} %step_ratio.1, s32[2,80]{1,0:T(2,128)} %mask_in.1, ...), custom_call_target="tpu_custom_call" | custom-call | tf_op jit(solution)/shard_map/pallas_call | solution.py:705
  180.8 0.0 copy-start
  180.8 2.2 %copy.21 = f32[2,152,640]{2,1,0:T(8,128)} copy(f32[2,152,640]{2,1,0:T(8,128)} %get-tuple-element.8) | data formatting | bytes 1556480
  183.0 2.1 %copy.22 = f32[2,152,640]{2,1,0:T(8,128)} copy(f32[2,152,640]{2,1,0:T(8,128)} %get-tuple-element.9) | data formatting | bytes 1556480
  185.0 2.1 %copy.23 = f32[2,152,640]{2,1,0:T(8,128)} copy(f32[2,152,640]{2,1,0:T(8,128)} %get-tuple-element.10) | data formatting | bytes 1556480
  187.1 0.0 copy-done
  187.1 1.7 copy.24
Async XLA Ops:
  180.8 6.3 %copy-start = (bf16[2,152,5120]{2,1,0:T(8,128)(2,1)S(1)}, bf16[2,152,5120]{2,1,0:T(8,128)(2,1)}, u32[]{:S(2)}) copy-start(bf16[2,152,5120]{2,1,0:T(8,128)(2,1)} %get-tuple-element.11) | copy-start | bytes 9338884

commit v2 on v1

--- a/solution.py
+++ b/solution.py
@@ -33,7 +33,7 @@
 OUT_COLS = ((0, 384), (384, 256))
 LAST = (((1,), (1,)), ((), ()))
 FIRST = (((0,), (0,)), ((), ()))
-N_COPIES = 180
+N_COPIES = 264
 
 
 def gelu_parts(pre):
@@ -46,13 +46,13 @@
 
 
 def kernel(
-    rewards,
-    group_ids,
-    step_index,
-    valid_steps,
-    step_ratio,
-    mask_in,
-    mod,
+    rewards_h,
+    group_ids_h,
+    step_index_h,
+    valid_steps_h,
+    step_ratio_h,
+    mask_h,
+    mod_h,
     lat_h,
     stale_h,
     noise_h,
@@ -80,16 +80,22 @@
     grad_own,
     b_send,
     b_recv,
-    lat,
     stale,
     noise,
     par,
     m1,
     m2,
-    fresh,
+    land,
     mask_col,
     stats,
     stats_recv,
+    rewards,
+    group_ids,
+    step_index,
+    valid_steps,
+    step_ratio,
+    mask_in,
+    mod,
     send_sem,
     recv_sem,
     local_sem,
@@ -119,7 +125,7 @@
     count = [0]
     sent = []
 
-    def push(src, dst, device, landed=None, keep=True):
+    def push(src, dst, device, landed=None, log=sent):
         i = count[0]
         count[0] += 1
         copy = pltpu.make_async_remote_copy(
@@ -131,8 +137,7 @@
             device_id_type=MESH,
         )
         copy.start()
-        if keep:
-            sent.append(copy)
+        log.append(copy)
         if landed is None:
             return copy
         return pltpu.make_async_remote_copy(
@@ -154,7 +159,15 @@
         return copy
 
     par_in = move(par_h, par)
-    lat_in = move(lat_h, lat)
+    lat_in = [move(lat_h.at[s], y_send.at[s, 0]) for s in range(2)] + [move(mod_h, mod)]
+    small_in = [
+        move(rewards_h, rewards),
+        move(group_ids_h, group_ids),
+        move(step_index_h, step_index),
+        move(valid_steps_h, valid_steps),
+        move(step_ratio_h, step_ratio),
+        move(mask_h, mask_in),
+    ]
     stale_in = move(stale_h, stale)
     noise_in = move(noise_h, noise)
     m1_in = move(m1_h, m1)
@@ -180,7 +193,7 @@
 
         def body(i, carry):
             rows = pl.ds(pl.multiple_of(i * CHUNK, CHUNK), CHUNK)
-            values = lat[s, rows, :].astype(F32)
+            values = y_send[s, 0, rows, :].astype(F32)
             middle = jnp.sum(values, axis=-1, keepdims=True) / D
             centred = values - middle
             spread = jnp.sum(centred * centred, axis=-1, keepdims=True) / D
@@ -192,15 +205,56 @@
 
     pl.semaphore_wait(barrier, len(partners))
 
-    first = {}
-    for m in range(2):
+    first, second, weights_sent = {}, {}, []
+
+    def near_own(m):
         for h in range(2):
             a, b = far_at[h], near_at[h]
             mine = raws[h].at[m, a, b]
-            first[m, h, 0] = push(mine, mine, near[h][1], raws[h].at[m, a, turn(b, 3)])
-            first[m, h, 1] = push(mine, mine, near[h][3], raws[h].at[m, a, turn(b, 1)])
-
-    lat_in.wait()
+            for k in (3, 1):
+                first[m, h, k] = push(
+                    mine, mine, near[h][4 - k], raws[h].at[m, a, turn(b, k)], weights_sent
+                )
+
+    def near_on(m):
+        k = (3, 1)[m]
+        for h in range(2):
+            a, b = far_at[h], near_at[h]
+            first[m, h, k].wait_recv()
+            block = raws[h].at[m, a, turn(b, k)]
+            first[m, h, 2] = push(
+                block, block, near[h][4 - k], raws[h].at[m, a, turn(b, 2)], weights_sent
+            )
+        for h in range(2):
+            first[m, h, 4 - k].wait_recv()
+
+    def far_own(m, k):
+        for h in range(2):
+            a, b = far_at[h], turn(near_at[h], k)
+            if k == 2:
+                first[m, h, 2].wait_recv()
+            block = raws[h].at[m, a, b]
+            for side in (3, 1):
+                second[m, h, k, side] = push(
+                    block, block, far[h][4 - side], raws[h].at[m, turn(a, side), b], weights_sent
+                )
+
+    def far_on(m, k):
+        side = 3 if k < 2 else 1
+        for h in range(2):
+            a, b = far_at[h], turn(near_at[h], k)
+            second[m, h, k, side].wait_recv()
+            block = raws[h].at[m, turn(a, side), b]
+            second[m, h, k, 2] = push(
+                block, block, far[h][4 - side], raws[h].at[m, turn(a, 2), b], weights_sent
+            )
+
+    near_own(0)
+    far_own(0, 0)
+    near_own(1)
+    far_own(1, 0)
+    for copy in lat_in:
+        copy.wait()
 
     def gather_own(buf, s):
         mine = buf.at[s, 0, 0]
@@ -237,10 +291,8 @@
         for j in range(4):
             d["sib%d" % j].wait_recv()
 
-    modulated(0)
-    rows0 = gather_own(hid, 0)
-    modulated(1)
-
+    for copy in small_in:
+        copy.wait()
     lane = lax.broadcasted_iota(jnp.int32, (1, 128), 1)
     valid = [jnp.where(step_index[s] < valid_steps[s], 1.0, 0.0).astype(F32) for s in range(2)]
     member = [jnp.where(lane == group_ids[s], 1.0, 0.0).astype(F32) for s in range(2)]
@@ -257,7 +309,7 @@
         copies = []
         for j in range(1, len(ring)):
             slot = stats_recv.at[step, j]
-            copies.append(push(stats, slot, ring[j], keep=False))
+            copies.append(push(stats, slot, ring[j], log=[]))
         return copies
 
     def stats_sum(step, copies):
@@ -269,50 +321,11 @@
             copy.wait_send()
         stats[...] = total
 
-    stats_copies = stats_send(0)
-
-    def pass_on(m):
-        for h in range(2):
-            a, b = far_at[h], near_at[h]
-            got = (turn(b, 3), turn(b, 1))[m]
-            step = (1, 3)[m]
-            first[m, h, m].wait_recv()
-            block = raws[h].at[m, a, got]
-            first[m, h, 2] = push(block, block, near[h][step], raws[h].at[m, a, turn(b, 2)])
-
-    second = {}
-
-    def groups(m):
-        for h in range(2):
-            first[m, h, 1 - m].wait_recv()
-            first[m, h, 2].wait_recv()
-            a = far_at[h]
-            lo, hi = (raws[h].at[m, a, pl.ds(k, 2)] for k in (0, 2))
-            left, right = turn(a, 3), turn(a, 1)
-            second[m, h, "left_lo"] = push(lo, lo, far[h][1], raws[h].at[m, left, pl.ds(0, 2)])
-            second[m, h, "right_hi"] = push(hi, hi, far[h][3], raws[h].at[m, right, pl.ds(2, 2)])
-            second[m, h, "left_hi"] = push(hi, hi, far[h][1], raws[h].at[m, left, pl.ds(2, 2)])
-            second[m, h, "right_lo"] = push(lo, lo, far[h][3], raws[h].at[m, right, pl.ds(0, 2)])
-
-    def groups_on(m):
-        for h in range(2):
-            a = far_at[h]
-            left, right, across = turn(a, 3), turn(a, 1), turn(a, 2)
-            second[m, h, "left_lo"].wait_recv()
-            block = raws[h].at[m, left, pl.ds(0, 2)]
-            second[m, h, "across_lo"] = push(
-                block, block, far[h][1], raws[h].at[m, across, pl.ds(0, 2)]
-            )
-            second[m, h, "right_hi"].wait_recv()
-            block = raws[h].at[m, right, pl.ds(2, 2)]
-            second[m, h, "across_hi"] = push(
-                block, block, far[h][3], raws[h].at[m, across, pl.ds(2, 2)]
-            )
-
     def assemble(m, out):
         for h in range(2):
-            for part in ("left_hi", "right_lo", "across_lo", "across_hi"):
-                second[m, h, part].wait_recv()
+            for k in range(4):
+                second[m, h, k, 1 if k < 2 else 3].wait_recv()
+                second[m, h, k, 2].wait_recv()
 
         def body(i, carry):
             base = pl.multiple_of(i * (4 * BLOCK), CHUNK)
@@ -323,23 +336,6 @@
             return carry
 
         lax.fori_loop(0, 4, body, 0)
-
-    pass_on(0)
-    pass_on(1)
-    gather_on(hid, 0, rows0)
-    groups(0)
-    rows1 = gather_own(hid, 1)
-    stats_sum(0, stats_copies)
-    stats_copies = stats_send(1)
-    gather_near(hid, 0, rows0)
-    groups_on(0)
-    groups(1)
-    stats_sum(1, stats_copies)
-    stats_copies = stats_send(2)
-    gather_end(hid, 0, rows0)
-    gather_on(hid, 1, rows1)
-    stats_sum(2, stats_copies)
-    stats_copies = stats_send(3)
 
     diag = lax.broadcasted_iota(jnp.int32, (PATCH, PATCH), 0) == lax.broadcasted_iota(
         jnp.int32, (PATCH, PATCH), 1
@@ -351,8 +347,6 @@
         mask_col[s] = jnp.broadcast_to(column, (PATCH, 128))
         npatch.append(jnp.maximum(jnp.sum(column, axis=0, keepdims=True), 1.0))
 
-    stats_sum(3, stats_copies)
-
     def forward(s):
         def body(i, carry):
             rows = hid[s, i].reshape(4 * PATCH, D)
@@ -363,14 +357,44 @@
 
         lax.fori_loop(0, 2, body, 0)
 
+    stats_copies = stats_send(0)
+    modulated(0)
+    stats_sum(0, stats_copies)
+    stats_copies = stats_send(1)
+    rows0 = gather_own(hid, 0)
+    near_on(0)
+    far_own(0, 3)
+    far_own(0, 1)
+    modulated(1)
+    rows1 = gather_own(hid, 1)
+    far_on(0, 0)
+    near_on(1)
+    gather_on(hid, 0, rows0)
+    far_on(1, 0)
+    far_own(0, 2)
+    far_own(1, 3)
+    far_own(1, 1)
+    far_on(0, 1)
+    far_on(0, 3)
+    stats_sum(1, stats_copies)
+    stats_copies = stats_send(2)
+    gather_near(hid, 0, rows0)
+    gather_on(hid, 1, rows1)
+    far_on(0, 2)
+    far_own(1, 2)
+    gather_end(hid, 0, rows0)
+    far_on(1, 1)
+    far_on(1, 3)
+    gather_near(hid, 1, rows1)
+    gather_sib(rows0)
     assemble(0, asm_up)
-    gather_sib(rows0)
     forward(0)
-    gather_near(hid, 1, rows1)
-    groups_on(1)
+    far_on(1, 2)
     gather_end(hid, 1, rows1)
     gather_sib(rows1)
     forward(1)
+    stats_sum(2, stats_copies)
+    stats_copies = stats_send(3)
     assemble(1, asm_down)
 
     def branch_tile(s, i, n):
@@ -432,8 +456,6 @@
             dst[k] = (dst[k].astype(F32) + src[k].astype(F32)).astype(BF)
 
     col_parts = tuple((lambda ref, k, cols=cols: ref.at[k, :, cols]) for cols in COLS)
-    block_parts = tuple((lambda ref, k, i=i: ref.at[k, pl.ds(i, 2)]) for i in (0, 2))
-    row_parts = tuple((lambda ref, k, r=r: ref.at[k, pl.ds(*r)]) for r in ((0, 48), (48, 32)))
 
     def branch_ring(s):
         return ring_start(y_send.at[s], y_recv.at[s], col_parts, y_plus, y_minus)
@@ -488,6 +510,7 @@
     branch_mine(1)
     branch_add(0, ring0)
     ring1 = branch_ring(1)
+    stats_sum(3, stats_copies)
     stale_in.wait()
     noise_in.wait()
     back_rows(0, ring0)
@@ -509,178 +532,240 @@
 
         lax.fori_loop(0, 2, body, 0)
 
-    def grad_tile(rows, s, n):
+    PARTS = ((1, 0, 256), (1, 256, 384), (0, 0, 384), (0, 384, 256))
+
+    def grad_part(p, rows, s, n):
         start, width = TILES[n]
         left = rows[s, :, :, :, start : start + width].reshape(8 * PATCH, width)
-        right = act[s].reshape(8 * PATCH, SLICE)
+        right = act[s, :, :, PARTS[p][1] : PARTS[p][1] + PARTS[p][2]].reshape(8 * PATCH, PARTS[p][2])
         return lax.dot_general(left, right, FIRST, preferred_element_type=F32)
 
-    def grad_rows(h, j, k):
+    def grad_rows(p, h, j, k):
         a, b = turn(far_at[h], j), turn(near_at[h], k)
         block = (b * 4 + a) if h == 0 else (a * 4 + b)
-        return grad[pl.ds(pl.multiple_of(block * BLOCK + 80 * h, 8), 80), :]
-
-    def far_start(m):
+        rows = pl.ds(pl.multiple_of(block * BLOCK + 80 * h, 8), 80)
+        return grad[rows, PARTS[p][1] : PARTS[p][1] + PARTS[p][2]]
+
+    def part_parts(p, lead):
+        cols = pl.ds(PARTS[p][1], PARTS[p][2])
+        if lead:
+            return tuple((lambda ref, k, i=i: ref.at[k, pl.ds(i, 2), :, cols]) for i in (0, 2))
+        return tuple((lambda ref, k, r=r: ref.at[k, pl.ds(*r), cols]) for r in ((0, 48), (48, 32)))
+
+    def far_ring(p, h):
+        m = PARTS[p][0]
+        return raws[h].at[m], x_recv.at[m, h], part_parts(p, True), far[h][1], far[h][3]
+
+    def near_ring(p, h):
+        m = PARTS[p][0]
+        return b_send.at[m, h], b_recv.at[m, h], part_parts(p, False), near[h][1], near[h][3]
+
+    def far_start(p):
+        m, start, width = PARTS[p]
+        cols = slice(start, start + width)
         for j, slot in ((2, 0), (1, 1), (3, 2)):
             for h in range(2):
                 for k in range(4):
-                    raws[h][m, slot, k] = grad_rows(h, j, k).astype(BF)
-        out = [
-            ring_start(raws[h].at[m], x_recv.at[m, h], block_parts, far[h][1], far[h][3])
-            for h in range(2)
-        ]
+                    raws[h][m, slot, k, :, cols] = grad_rows(p, h, j, k).astype(BF)
+        out = [ring_start(*far_ring(p, h)) for h in range(2)]
         for h in range(2):
             for k in range(4):
-                grad_own[m, h, k] = grad_rows(h, 0, k)
+                grad_own[m, h, k, :, cols] = grad_rows(p, h, 0, k)
         return out
 
-    def far_add(m, d):
-        for h in range(2):
-            ring_add(
-                raws[h].at[m],
-                x_recv.at[m, h],
-                block_parts,
-                far[h][1],
-                far[h][3],
-                add_blocks,
-                d[h],
-            )
-
-    def near_start(m, d):
+    def far_add(p, d):
+        for h in range(2):
+            ring_add(*far_ring(p, h), add_blocks, d[h])
+
+    def near_start(p, d):
+        m, start, width = PARTS[p]
+        cols = slice(start, start + width)
         out = []
         for h in range(2):
             ring_wait(d[h])
             for k in (2, 1, 3, 0):
                 total = (
-                    grad_own[m, h, k] + x_recv[m, h, 1, k].astype(F32) + x_recv[m, h, 2, k].astype(F32)
+                    grad_own[m, h, k, :, cols]
+                    + x_recv[m, h, 1, k, :, cols].astype(F32)
+                    + x_recv[m, h, 2, k, :, cols].astype(F32)
                 )
                 if k == 0:
-                    grad_own[m, h, 0] = total
+                    grad_own[m, h, 0, :, cols] = total
                 else:
-                    b_send[m, h, {2: 0, 1: 1, 3: 2}[k]] = total.astype(BF)
-            out.append(
-                ring_start(b_send.at[m, h], b_recv.at[m, h], row_parts, near[h][1], near[h][3])
-            )
+                    b_send[m, h, {2: 0, 1: 1, 3: 2}[k], :, cols] = total.astype(BF)
+            out.append(ring_start(*near_ring(p, h)))
         return out
 
-    def near_add(m, d):
-        for h in range(2):
-            ring_add(
-                b_send.at[m, h],
-                b_recv.at[m, h],
-                row_parts,
-                near[h][1],
-                near[h][3],
-                add_rows,
-                d[h],
-            )
+    def near_add(p, d):
+        for h in range(2):
+            ring_add(*near_ring(p, h), add_rows, d[h])
 
     def out_cols(owner, start, width):
         return pl.ds(pl.multiple_of(owner * SLICE + start, 128), width)
 
     out_copies = []
 
-    def update(m, d):
+    def update(p, d):
+        m, start, width = PARTS[p]
+        cols = slice(start, start + width)
         for h in range(2):
             ring_wait(d[h])
             rows = slice(0, 80) if h == 0 else slice(80, BLOCK)
             high = 80 if h == 0 else 72
             grads = (
-                grad_own[m, h, 0, 0:high, :]
-                + b_recv[m, h, 1, 0:high, :].astype(F32)
-                + b_recv[m, h, 2, 0:high, :].astype(F32)
+                grad_own[m, h, 0, 0:high, cols]
+                + b_recv[m, h, 1, 0:high, cols].astype(F32)
+                + b_recv[m, h, 2, 0:high, cols].astype(F32)
             )
-            weights = par[m, rows, :]
-            new_first = beta_one * m1[m, rows, :] + (1.0 - beta_one) * grads
-            new_second = beta_two * m2[m, rows, :] + (1.0 - beta_two) * grads * grads
+            weights = par[m, rows, cols]
+            new_first = beta_one * m1[m, rows, cols] + (1.0 - beta_one) * grads
+            new_second = beta_two * m2[m, rows, cols] + (1.0 - beta_two) * grads * grads
             first_hat = new_first / (1.0 - beta_one**adam_count)
             second_hat = new_second / (1.0 - beta_two**adam_count)
             step = first_hat / (jnp.sqrt(second_hat) + adam_eps) + weight_decay * weights
             new_weights = weights - learn_rate * step
-            m1[m, rows, :] = new_first
-            m2[m, rows, :] = new_second
-            par[m, rows, :] = new_weights
-            fresh[m, rows, :] = new_weights.astype(BF)
-        d = {}
-        place = o_roll.at[m, :, out_cols(roll, 0, SLICE)]
-        left = o_roll.at[m, :, out_cols(turn(y, 3) * 2 + c, 0, SLICE)]
-        right = o_roll.at[m, :, out_cols(turn(y, 1) * 2 + c, 0, SLICE)]
-        d["left"] = push(fresh.at[m], place, y_plus, left)
-        d["right"] = push(fresh.at[m], place, y_minus, right)
-        other = o_roll.at[m, :, out_cols(y * 2 + 1 - c, 0, SLICE)]
-        d["sib0"] = push(fresh.at[m], place, sibling, other)
-        out_copies.append(move(fresh.at[m], place))
-        out_copies.append(move(m1.at[m], o_m1.at[m]))
-        out_copies.append(move(m2.at[m], o_m2.at[m]))
-        out_copies.append(move(par.at[m], o_par.at[m]))
+            m1[m, rows, cols] = new_first
+            m2[m, rows, cols] = new_second
+            par[m, rows, cols] = new_weights
+            land[m, 0, rows, cols] = new_weights.astype(BF)
+        mine = land.at[m, 0, :, pl.ds(start, width)]
+
+        def slot(j, k):
+            return land.at[m, 2 * j + k, :, pl.ds(start, width)]
+
+        d = {
+            "left": push(mine, slot(3, 0), y_plus),
+            "right": push(mine, slot(1, 0), y_minus),
+            "sib0": push(mine, slot(0, 1), sibling),
+        }
+        out_store(p, 0, 0)
+        if p in (1, 3):
+            out_copies.append(move(m1.at[m], o_m1.at[m]))
+            out_copies.append(move(m2.at[m], o_m2.at[m]))
+            out_copies.append(move(par.at[m], o_par.at[m]))
         return d
 
-    def out_on(m, d):
-        across = turn(y, 2)
-        for key, by, to, half in (("left", 3, y_plus, 0), ("right", 1, y_minus, 1)):
-            owner = turn(y, by)
+    def out_store(p, j, k):
+        m, start, width = PARTS[p]
+        owner = turn(y, j) * 2 + (c if k == 0 else 1 - c)
+        block = land.at[m, 2 * j + k, :, pl.ds(start, width)]
+        out_copies.append(move(block, o_roll.at[m, :, out_cols(owner, start, width)]))
+
+    def out_on(p, d):
+        m, start, width = PARTS[p]
+        half = 128 * ((width // 128 + 1) // 2)
+        for key, j, to, at_, wide in (
+            ("left", 3, y_plus, start, half),
+            ("right", 1, y_minus, start + half, width - half),
+        ):
             d[key].wait_recv()
-            start, width = OUT_COLS[half]
-            block = o_roll.at[m, :, out_cols(owner * 2 + c, start, width)]
-            landed = o_roll.at[m, :, out_cols(across * 2 + c, start, width)]
-            d[key, "across"] = push(block, block, to, landed)
-            whole = o_roll.at[m, :, out_cols(owner * 2 + c, 0, SLICE)]
-            twin = o_roll.at[m, :, out_cols(owner * 2 + 1 - c, 0, SLICE)]
-            d[key, "sib"] = push(whole, whole, sibling, twin)
-
-    def out_end(m, d):
-        across = turn(y, 2)
+            cols = pl.ds(at_, wide)
+            d[key, "across"] = push(land.at[m, 2 * j, :, cols], land.at[m, 4, :, cols], to)
+            cols = pl.ds(start, width)
+            d[key, "sib"] = push(
+                land.at[m, 2 * j, :, cols], land.at[m, 2 * j + 1, :, cols], sibling
+            )
+            out_store(p, j, 0)
+
+    def out_end(p, d):
+        m, start, width = PARTS[p]
         d["left", "across"].wait_recv()
         d["right", "across"].wait_recv()
-        whole = o_roll.at[m, :, out_cols(across * 2 + c, 0, SLICE)]
-        twin = o_roll.at[m, :, out_cols(across * 2 + 1 - c, 0, SLICE)]
-        d["sib2"] = push(whole, whole, sibling, twin)
-
-    def out_sib(d):
+        cols = pl.ds(start, width)
+        d["sib2"] = push(land.at[m, 4, :, cols], land.at[m, 5, :, cols], sibling)
+        out_store(p, 2, 0)
+
+    def out_sib(p, d):
         d["sib0"].wait_recv()
+        out_store(p, 0, 1)
         d["left", "sib"].wait_recv()
+        out_store(p, 3, 1)
         d["right", "sib"].wait_recv()
+        out_store(p, 1, 1)
         d["sib2"].wait_recv()
-
-    for copy in sent:
+        out_store(p, 2, 1)
+
+    for copy in weights_sent:
         copy.wait_send()
-    sent.clear()
     grad[pl.ds(D, 8), :] = jnp.zeros((8, SLICE), F32)
 
     for n, (start, width) in enumerate(TILES):
-        grad[start : start + width, :] = grad_tile(bk, 0, n)
+        for p in (0, 1):
+            cols = slice(PARTS[p][1], PARTS[p][1] + PARTS[p][2])
+            grad[start : start + width, cols] = grad_part(p, bk, 0, n)
     gather_on(bk, 1, back1)
     back_pre(0)
     gather_near(bk, 1, back1)
     gather_end(bk, 1, back1)
     gather_sib(back1)
-    for n, (start, width) in enumerate(TILES):
-        grad[start : start + width, :] += grad_tile(bk, 1, n)
-    down_far = far_start(1)
+
+    def down_part(p):
+        cols = slice(PARTS[p][1], PARTS[p][1] + PARTS[p][2])
+        for n, (start, width) in enumerate(TILES):
+            grad[start : start + width, cols] += grad_part(p, bk, 1, n)
+
+    def up_part(p):
+        cols = slice(PARTS[p][1], PARTS[p][1] + PARTS[p][2])
+        for n, (start, width) in enumerate(TILES):
+            grad[start : start + width, cols] = grad_part(p, hid, 0, n) + grad_part(p, hid, 1, n)
+
+    down_part(0)
+    far0 = far_start(0)
+    down_part(1)
+    far1 = far_start(1)
     back_pre(1)
-    far_add(1, down_far)
-    for n, (start, width) in enumerate(TILES):
-        grad[start : start + width, :] = grad_tile(hid, 0, n) + grad_tile(hid, 1, n)
-    up_far = far_start(0)
+    far_add(0, far0)
+    up_part(2)
+    far_add(1, far1)
+    far2 = far_start(2)
+    up_part(3)
     m1_in.wait()
     m2_in.wait()
-    down_near = near_start(1, down_far)
-    far_add(0, up_far)
-    near_add(1, down_near)
-    down_out = update(1, down_near)
-    out_on(1, down_out)
-    up_near = near_start(0, up_far)
-    near_add(0, up_near)
-    out_end(1, down_out)
-    up_out = update(0, up_near)
-    out_on(0, up_out)
-    out_sib(down_out)
-    out_end(0, up_out)
-    out_sib(up_out)
+    near0 = near_start(0, far0)
+    near1 = near_start(1, far1)
+    far3 = far_start(3)
+    far_add(2, far2)
+    near_add(0, near0)
+    near_add(1, near1)
+    far_add(3, far3)
+    out0 = update(0, near0)
+    near2 = near_start(2, far2)
+    out1 = update(1, near1)
+    near3 = near_start(3, far3)
+    near_add(2, near2)
+    near_add(3, near3)
+    out_on(0, out0)
+    out2 = update(2, near2)
+    out3 = update(3, near3)
+    out_on(1, out1)
+    out_end(0, out0)
+    out_on(2, out2)
+    out_end(1, out1)
+    out_on(3, out3)
+    out_end(2, out2)
+    out_end(3, out3)
+    for p, out in enumerate((out0, out1, out2, out3)):
+        out_sib(p, out)
     for copy in out_copies:
         copy.wait()
     for copy in sent:
         copy.wait_send()
+
+
+def settle(*refs):
+    sources, targets, held, sem = refs[:4], refs[4:8], refs[8:12], refs[12]
+    pieces = [(i, m) for i in range(4) for m in range(2)]
+    reads = []
+    for n, (i, m) in enumerate(pieces):
+        reads.append(pltpu.make_async_copy(sources[i].at[m], held[i].at[m], sem.at[n]))
+        reads[-1].start()
+    writes = []
+    for n, (i, m) in enumerate(pieces):
+        reads[n].wait()
+        writes.append(pltpu.make_async_copy(held[i].at[m], targets[i].at[m], sem.at[8 + n]))
+        writes[-1].start()
+    for write in writes:
+        write.wait()
 
 
 def per_device(
@@ -699,13 +784,11 @@
     second_moment,
 ):
     any_ = pl.BlockSpec(memory_space=pl.ANY)
-    smem = pl.BlockSpec(memory_space=pltpu.SMEM)
-    vmem = pl.BlockSpec(memory_space=pltpu.VMEM)
     shard = jax.ShapeDtypeStruct(params.shape, F32)
     outs = pl.pallas_call(
         kernel,
         out_shape=(shard, shard, shard, jax.ShapeDtypeStruct((2, BLOCK, 8 * SLICE), BF)),
-        in_specs=[smem] * 5 + [vmem] * 2 + [any_] * 6,
+        in_specs=[any_] * 13,
         out_specs=(any_,) * 4,
         scratch_shapes=[
             pltpu.VMEM((2, 2, 4, PATCH, D), BF),
@@ -727,17 +810,23 @@
             pltpu.VMEM((2, 2, 3, 80, SLICE), BF),
             pltpu.VMEM((2, PATCH, D), BF),
             pltpu.VMEM((2, PATCH, D), BF),
-            pltpu.VMEM((2, PATCH, D), BF),
             pltpu.VMEM((2, BLOCK, SLICE), F32),
             pltpu.VMEM((2, BLOCK, SLICE), F32),
             pltpu.VMEM((2, BLOCK, SLICE), F32),
-            pltpu.VMEM((2, BLOCK, SLICE), BF),
+            pltpu.VMEM((2, 8, BLOCK, SLICE), BF),
             pltpu.VMEM((2, PATCH, 128), F32),
             pltpu.VMEM((8, 128), F32),
             pltpu.VMEM((4, 4, 8, 128), F32),
+            pltpu.SMEM((2,), F32),
+            pltpu.SMEM((2,), jnp.int32),
+            pltpu.SMEM((2,), jnp.int32),
+            pltpu.SMEM((2,), jnp.int32),
+            pltpu.SMEM((2,), F32),
+            pltpu.VMEM((2, PATCH), jnp.int32),
+            pltpu.VMEM((3, 2, D), F32),
             pltpu.SemaphoreType.DMA((N_COPIES,)),
             pltpu.SemaphoreType.DMA((N_COPIES,)),
-            pltpu.SemaphoreType.DMA((16,)),
+            pltpu.SemaphoreType.DMA((56,)),
         ],
         compiler_params=pltpu.CompilerParams(
             collective_id=0, has_side_effects=True, vmem_limit_bytes=63 << 20
@@ -757,7 +846,16 @@
         first_moment,
         second_moment,
     )
-    return tuple(outs)
+    return tuple(
+        pl.pallas_call(
+            settle,
+            out_shape=tuple(jax.ShapeDtypeStruct(o.shape, o.dtype) for o in outs),
+            in_specs=[any_] * 4,
+            out_specs=(any_,) * 4,
+            scratch_shapes=[pltpu.VMEM(o.shape, o.dtype) for o in outs]
+            + [pltpu.SemaphoreType.DMA((16,))],
+        )(*outs)
+    )
 
 
 def solution(mesh):

time: 190 us -> 169 us (0.89)
  Pallas kernels: 180 us -> 168 us
  local copies, waits for them, and re-layouts: 7.98 us -> 0 us
    pallas_call x1, Pallas kernels: 180 us -> 163 us  [per_device(): pl.pallas_call(kernel, out_shape=(shard, shard, shard, jax.ShapeDtypeStru...]
    unnamed x6 -> x0, local copies, waits for them, and re-layouts: 7.98 us -> none
    pallas_call x0 -> x1, Pallas kernels: none -> 4.71 us  [per_device(): pl.pallas_call(settle, out_shape=tuple((jax.ShapeDtypeStruct(o.shape, o.d...]
where the time goes in v2:
time: 169 us
  Pallas kernels  168 us (99%)
    pallas_call x1, Pallas kernels, per_device(): pl.pallas_call(kernel, out_shape=(shard, shard, shard, jax.ShapeDtypeStru...  163 us
    pallas_call x1, Pallas kernels, per_device(): pl.pallas_call(settle, out_shape=tuple((jax.ShapeDtypeStruct(o.shape, o.d...  4.71 us

profile of v2, /device:TPU:1, one launch (start us, length us, event | category | flops | bytes accessed | tf_op | source)
XLA Modules:
  0.0 168.8 jit_solution(14798265504948266119)
XLA Ops:
  0.6 163.3 %shard_map.156 = (f32[2,152,640]{2,1,0:T(8,128)}, f32[2,152,640]{2,1,0:T(8,128)}, f32[2,152,640]{2,1,0:T(8,128)}, bf16[2,152,5120]{2,1,0:T(8,128)(2,1)}) custom-call(f32[2]{0:T(128)} %rewards_h.1, s32[2]{0:T(128)} %group_ids_h.1, s32[2]{0:T(128)} %step_index_h.1, s32[2]{0:T(128)} %valid_steps_h.1, f32[2]{0:T(128)} %step_ratio_h.1, s32[2,80]{1,0:T(2,128)} %mask_h.1, ...), custom_call_target="tpu_custom_call" | custom-call | tf_op jit(solution)/shard_map/pallas_call | solution.py:788
  163.9 4.7 %shard_map.157 = (f32[2,152,640]{2,1,0:T(8,128)}, f32[2,152,640]{2,1,0:T(8,128)}, f32[2,152,640]{2,1,0:T(8,128)}, bf16[2,152,5120]{2,1,0:T(8,128)(2,1)}) custom-call(f32[2,152,640]{2,1,0:T(8,128)} %get-tuple-element.8.refs_0_, f32[2,152,640]{2,1,0:T(8,128)} %get-tuple-element.9.refs_1_, f32[2,152,640]{2,1,0:T(8,128)} %get-tuple-element.10.refs_2_, ...), custom_call_target="tpu_custom_call" | custom-call | tf_op jit(solution)/shard_map/pallas_call | solution.py:850

commit v3 on v2

--- a/solution.py
+++ b/solution.py
@@ -28,12 +28,14 @@
 BF = jnp.bfloat16
 F32 = jnp.float32
 MESH = pl.DeviceIdType.MESH
-TILES = ((0, 640), (640, 640), (1280, 640), (1920, 512))
 COLS = (pl.ds(0, 1280), pl.ds(1280, 1152))
 OUT_COLS = ((0, 384), (384, 256))
 LAST = (((1,), (1,)), ((), ()))
 FIRST = (((0,), (0,)), ((), ()))
-N_COPIES = 264
+N_SEND = 48
+N_PAIR = 8
+N_RECV = 141
+N_LOCAL = 20
 
 
 def gelu_parts(pre):
@@ -43,6 +45,16 @@
     cdf = 0.5 * (1.0 + t)
     slope = cdf + pre * (0.5 * (1.0 - t * t)) * (root * (1.0 + (3.0 * 0.044715) * square))
     return pre * cdf, slope
+
+
+class Once:
+    def __init__(self, wait):
+        self.todo = wait
+
+    def wait(self):
+        if self.todo is not None:
+            self.todo()
+        self.todo = None
 
 
 def kernel(
@@ -122,41 +134,46 @@
     for partner in partners:
         pl.semaphore_signal(barrier, inc=1, device_id=partner, device_id_type=MESH)
 
-    count = [0]
-    sent = []
-
-    def push(src, dst, device, landed=None, log=sent):
-        i = count[0]
-        count[0] += 1
-        copy = pltpu.make_async_remote_copy(
-            src_ref=src,
-            dst_ref=dst,
-            send_sem=send_sem.at[i],
-            recv_sem=recv_sem.at[i],
-            device_id=device,
-            device_id_type=MESH,
-        )
+    stage, fresh_id, spare, sends, moves = [0], [0], [], [], []
+
+    def recv_id():
+        if stage[0] == 2 and spare:
+            return spare.pop(0)
+        fresh_id[0] += 1
+        if stage[0] == 0:
+            spare.append(fresh_id[0] - 1)
+        return fresh_id[0] - 1
+
+    def push(src, dst, device, landed=None, log=None):
+        i, n = recv_id(), len(sends)
+        if n >= N_SEND:
+            sends[n - N_SEND].wait()
+
+        def describe(src, dst):
+            return pltpu.make_async_remote_copy(
+                src_ref=src,
+                dst_ref=dst,
+                send_sem=send_sem.at[n % N_SEND],
+                recv_sem=recv_sem.at[i],
+                device_id=device,
+                device_id_type=MESH,
+            )
+
+        copy = describe(src, dst)
         copy.start()
-        log.append(copy)
-        if landed is None:
-            return copy
-        return pltpu.make_async_remote_copy(
-            src_ref=landed,
-            dst_ref=landed,
-            send_sem=send_sem.at[i],
-            recv_sem=recv_sem.at[i],
-            device_id=device,
-            device_id_type=MESH,
-        )
-
-    local = [0]
+        sends.append(Once(copy.wait_send))
+        if log is not None:
+            log.append(sends[-1])
+        return copy if landed is None else describe(landed, landed)
 
     def move(src, dst):
-        i = local[0]
-        local[0] += 1
-        copy = pltpu.make_async_copy(src, dst, local_sem.at[i])
+        n = len(moves)
+        if n >= N_LOCAL:
+            moves[n - N_LOCAL].wait()
+        copy = pltpu.make_async_copy(src, dst, local_sem.at[n % N_LOCAL])
         copy.start()
-        return copy
+        moves.append(Once(copy.wait))
+        return moves[-1]
 
     par_in = move(par_h, par)
     lat_in = [move(lat_h.at[s], y_send.at[s, 0]) for s in range(2)] + [move(mod_h, mod)]
@@ -168,10 +185,6 @@
         move(step_ratio_h, step_ratio),
         move(mask_h, mask_in),
     ]
-    stale_in = move(stale_h, stale)
-    noise_in = move(noise_h, noise)
-    m1_in = move(m1_h, m1)
-    m2_in = move(m2_h, m2)
 
     raws = (raw0, raw1)
     near = (x_ring, z_ring)
@@ -186,6 +199,13 @@
         raw1[m, x, z, 64:80, :] = jnp.concatenate(
             [par[m, 144:BLOCK, :], jnp.zeros((8, SLICE), F32)], axis=0
         ).astype(BF)
+
+    def each(n, body):
+        def step(i, carry):
+            body(i)
+            return carry
+
+        lax.fori_loop(0, n, step, 0)
 
     def modulated(s):
         shift = mod[0, s : s + 1, :]
@@ -213,7 +233,7 @@
             mine = raws[h].at[m, a, b]
             for k in (3, 1):
                 first[m, h, k] = push(
-                    mine, mine, near[h][4 - k], raws[h].at[m, a, turn(b, k)], weights_sent
+                    mine, mine, near[h][4 - k], raws[h].at[m, a, turn(b, k)], log=weights_sent
                 )
 
     def near_on(m):
@@ -223,7 +243,7 @@
             first[m, h, k].wait_recv()
             block = raws[h].at[m, a, turn(b, k)]
             first[m, h, 2] = push(
-                block, block, near[h][4 - k], raws[h].at[m, a, turn(b, 2)], weights_sent
+                block, block, near[h][4 - k], raws[h].at[m, a, turn(b, 2)], log=weights_sent
             )
         for h in range(2):
             first[m, h, 4 - k].wait_recv()
@@ -236,7 +256,7 @@
             block = raws[h].at[m, a, b]
             for side in (3, 1):
                 second[m, h, k, side] = push(
-                    block, block, far[h][4 - side], raws[h].at[m, turn(a, side), b], weights_sent
+                    block, block, far[h][4 - side], raws[h].at[m, turn(a, side), b], log=weights_sent
                 )
 
     def far_on(m, k):
@@ -246,13 +266,14 @@
             second[m, h, k, side].wait_recv()
             block = raws[h].at[m, turn(a, side), b]
             second[m, h, k, 2] = push(
-                block, block, far[h][4 - side], raws[h].at[m, turn(a, 2), b], weights_sent
+                block, block, far[h][4 - side], raws[h].at[m, turn(a, 2), b], log=weights_sent
             )
 
     near_own(0)
-    far_own(0, 0)
-    near_own(1)
-    far_own(1, 0)
+    stale_in = move(stale_h, stale)
+    noise_in = move(noise_h, noise)
+    m1_in = move(m1_h, m1)
+    m2_in = move(m2_h, m2)
     for copy in lat_in:
         copy.wait()
 
@@ -290,6 +311,52 @@
     def gather_sib(d):
         for j in range(4):
             d["sib%d" % j].wait_recv()
+
+    def stats_send(step):
+        ring = ([None, sibling], y_ring, x_ring, z_ring)[step]
+        log = []
+        return [
+            push(stats, stats_recv.at[step, j], ring[j], log=log) for j in range(1, len(ring))
+        ], log
+
+    def stats_sum(step, copies):
+        total = stats[...]
+        for j, copy in enumerate(copies[0]):
+            copy.wait_recv()
+            total = total + stats_recv[step, j + 1]
+        for copy in copies[1]:
+            copy.wait()
+        stats[...] = total
+
+    def assemble(m, out):
+        for h in range(2):
+            for k in range(4):
+                second[m, h, k, 1 if k < 2 else 3].wait_recv()
+                second[m, h, k, 2].wait_recv()
+
+        def body(i, carry):
+            base = pl.multiple_of(i * (4 * BLOCK), CHUNK)
+            parts = []
+            for k in range(4):
+                parts += [raw0[m, k, i], raw1[m, i, k, 0:72, :]]
+            out[pl.ds(base, 4 * BLOCK), :] = jnp.concatenate(parts, axis=0)
+            return carry
+
+        lax.fori_loop(0, 4, body, 0)
+
+    def forward(s, i):
+        rows = hid[s, i].reshape(4 * PATCH, D)
+        value = jnp.dot(rows, asm_up[0:D, :], preferred_element_type=F32)
+        pre[s, i] = value
+        act[s, i] = gelu_parts(value)[0].astype(BF)
+
+    modulated(0)
+    rows0 = gather_own(hid, 0)
+    near_own(1)
+    near_on(0)
+    far_own(0, 1)
+    far_own(0, 0)
+    modulated(1)
 
     for copy in small_in:
         copy.wait()
@@ -304,122 +371,76 @@
     )
     stats[3:4, :] = jnp.zeros((1, 128), F32) + (valid[0] + valid[1])
 
-    def stats_send(step):
-        ring = ([None, sibling], y_ring, x_ring, z_ring)[step]
-        copies = []
-        for j in range(1, len(ring)):
-            slot = stats_recv.at[step, j]
-            copies.append(push(stats, slot, ring[j], log=[]))
-        return copies
-
-    def stats_sum(step, copies):
-        total = stats[...]
-        for j, copy in enumerate(copies):
-            copy.wait_recv()
-            total = total + stats_recv[step, j + 1]
-        for copy in copies:
-            copy.wait_send()
-        stats[...] = total
-
-    def assemble(m, out):
-        for h in range(2):
-            for k in range(4):
-                second[m, h, k, 1 if k < 2 else 3].wait_recv()
-                second[m, h, k, 2].wait_recv()
-
-        def body(i, carry):
-            base = pl.multiple_of(i * (4 * BLOCK), CHUNK)
-            parts = []
-            for k in range(4):
-                parts += [raw0[m, k, i], raw1[m, i, k, 0:72, :]]
-            out[pl.ds(base, 4 * BLOCK), :] = jnp.concatenate(parts, axis=0)
-            return carry
-
-        lax.fori_loop(0, 4, body, 0)
-
-    diag = lax.broadcasted_iota(jnp.int32, (PATCH, PATCH), 0) == lax.broadcasted_iota(
-        jnp.int32, (PATCH, PATCH), 1
-    )
-    npatch = []
-    for s in range(2):
-        row = jnp.broadcast_to(mask_in[s : s + 1, :].astype(F32), (PATCH, PATCH))
-        column = jnp.sum(jnp.where(diag, row, 0.0), axis=1, keepdims=True)
-        mask_col[s] = jnp.broadcast_to(column, (PATCH, 128))
-        npatch.append(jnp.maximum(jnp.sum(column, axis=0, keepdims=True), 1.0))
-
-    def forward(s):
-        def body(i, carry):
-            rows = hid[s, i].reshape(4 * PATCH, D)
-            value = jnp.dot(rows, asm_up[0:D, :], preferred_element_type=F32)
-            pre[s, i] = value
-            act[s, i] = gelu_parts(value)[0].astype(BF)
-            return carry
-
-        lax.fori_loop(0, 2, body, 0)
-
     stats_copies = stats_send(0)
-    modulated(0)
+    gather_on(hid, 0, rows0)
+    near_on(1)
+    rows1 = gather_own(hid, 1)
     stats_sum(0, stats_copies)
+    far_own(0, 3)
+    far_own(0, 2)
+    far_on(0, 1)
+    far_own(1, 2)
+    far_on(0, 2)
+    far_on(0, 0)
+    far_on(0, 3)
+    far_own(1, 0)
+    far_own(1, 3)
+    gather_on(hid, 1, rows1)
     stats_copies = stats_send(1)
-    rows0 = gather_own(hid, 0)
-    near_on(0)
-    far_own(0, 3)
-    far_own(0, 1)
-    modulated(1)
-    rows1 = gather_own(hid, 1)
-    far_on(0, 0)
-    near_on(1)
-    gather_on(hid, 0, rows0)
+    gather_near(hid, 0, rows0)
+    gather_end(hid, 0, rows0)
+    far_on(1, 2)
+    far_own(1, 1)
+    assemble(0, asm_up)
+    gather_sib(rows0)
+    forward(0, 0)
+    gather_near(hid, 1, rows1)
     far_on(1, 0)
-    far_own(0, 2)
-    far_own(1, 3)
-    far_own(1, 1)
-    far_on(0, 1)
-    far_on(0, 3)
+    forward(0, 1)
+    gather_end(hid, 1, rows1)
+    far_on(1, 3)
+    far_on(1, 1)
+    gather_sib(rows1)
+    each(2, lambda i: forward(1, i))
+    assemble(1, asm_down)
+    stage[0] = 1
     stats_sum(1, stats_copies)
     stats_copies = stats_send(2)
-    gather_near(hid, 0, rows0)
-    gather_on(hid, 1, rows1)
-    far_on(0, 2)
-    far_own(1, 2)
-    gather_end(hid, 0, rows0)
-    far_on(1, 1)
-    far_on(1, 3)
-    gather_near(hid, 1, rows1)
-    gather_sib(rows0)
-    assemble(0, asm_up)
-    forward(0)
-    far_on(1, 2)
-    gather_end(hid, 1, rows1)
-    gather_sib(rows1)
-    forward(1)
-    stats_sum(2, stats_copies)
-    stats_copies = stats_send(3)
-    assemble(1, asm_down)
+
+    def pair_copy(s, n):
+        i = s * 4 + n
+        return pltpu.make_async_remote_copy(
+            src_ref=asm_up.at[pl.ds(pl.multiple_of((s * 4 + n) * 320, CHUNK), 320)],
+            dst_ref=sib_recv.at[s, n],
+            send_sem=send_sem.at[N_SEND + i],
+            recv_sem=recv_sem.at[N_RECV + i],
+            device_id=sibling,
+            device_id_type=MESH,
+        )
 
     def branch_tile(s, i, n):
-        start, width = TILES[n]
-        return lax.dot_general(
-            act[s, i], asm_down[start : start + width, :], LAST, preferred_element_type=F32
-        )
-
-    pair = {}
+        cols = pl.ds(pl.multiple_of(jnp.minimum(n * SLICE, D - SLICE), 128), SLICE)
+        value = lax.dot_general(act[s, i], asm_down[cols, :], LAST, preferred_element_type=F32)
+        return cols, value
 
     def branch_away(s):
-        for n, (start, width) in enumerate(TILES):
-            slot = asm_up.at[pl.ds((s * 4 + n) * 320, 320)]
-            slot[:, 0:width] = branch_tile(s, 1, n).astype(BF)
-            pair[s, n] = push(slot, sib_recv.at[s, n], sibling)
+        def body(n):
+            value = branch_tile(s, 1, n)[1]
+            asm_up[pl.ds(pl.multiple_of((s * 4 + n) * 320, CHUNK), 320), :] = value.astype(BF)
+            pair_copy(s, n).start()
+
+        each(4, body)
 
     def branch_mine(s):
-        for n, (start, width) in enumerate(TILES):
-            value = branch_tile(s, 0, n)
-            pair[s, n].wait_recv()
-            value = value + sib_recv[s, n, :, 0:width].astype(F32)
-            cols = slice(start, start + width)
+        def body(n):
+            cols, value = branch_tile(s, 0, n)
+            pair_copy(s, n).wait()
+            value = value + sib_recv[s, n].astype(F32)
             own[s, :, cols] = value[0:80]
             for j, k in ((2, 0), (1, 1), (3, 2)):
                 y_send[s, k, :, cols] = value[j * 80 : j * 80 + 80].astype(BF)
+
+        each(4, body)
 
     def ring_start(send, recv, parts, plus, minus):
         lo, hi = parts
@@ -506,6 +527,19 @@
     branch_away(0)
     branch_mine(0)
     ring0 = branch_ring(0)
+    stats_sum(2, stats_copies)
+    stats_copies = stats_send(3)
+
+    diag = lax.broadcasted_iota(jnp.int32, (PATCH, PATCH), 0) == lax.broadcasted_iota(
+        jnp.int32, (PATCH, PATCH), 1
+    )
+    npatch = []
+    for s in range(2):
+        row = jnp.broadcast_to(mask_in[s : s + 1, :].astype(F32), (PATCH, PATCH))
+        column = jnp.sum(jnp.where(diag, row, 0.0), axis=1, keepdims=True)
+        mask_col[s] = jnp.broadcast_to(column, (PATCH, 128))
+        npatch.append(jnp.maximum(jnp.sum(column, axis=0, keepdims=True), 1.0))
+
     branch_away(1)
     branch_mine(1)
     branch_add(0, ring0)
@@ -515,6 +549,7 @@
     noise_in.wait()
     back_rows(0, ring0)
     branch_add(1, ring1)
+    stage[0] = 2
     back0 = gather_own(bk, 0)
     back_rows(1, ring1)
     gather_on(bk, 0, back0)
@@ -534,10 +569,13 @@
 
     PARTS = ((1, 0, 256), (1, 256, 384), (0, 0, 384), (0, 384, 256))
 
-    def grad_part(p, rows, s, n):
-        start, width = TILES[n]
-        left = rows[s, :, :, :, start : start + width].reshape(8 * PATCH, width)
-        right = act[s, :, :, PARTS[p][1] : PARTS[p][1] + PARTS[p][2]].reshape(8 * PATCH, PARTS[p][2])
+    def over_width(body):
+        each(3, lambda n: body(pl.multiple_of(n * SLICE, 128), SLICE))
+        body(3 * SLICE, D - 3 * SLICE)
+
+    def grad_part(rows, s, at_, wide, start, width):
+        left = rows[s, :, :, :, pl.ds(at_, wide)].reshape(8 * PATCH, wide)
+        right = act[s, :, :, start : start + width].reshape(8 * PATCH, width)
         return lax.dot_general(left, right, FIRST, preferred_element_type=F32)
 
     def grad_rows(p, h, j, k):
@@ -546,31 +584,30 @@
         rows = pl.ds(pl.multiple_of(block * BLOCK + 80 * h, 8), 80)
         return grad[rows, PARTS[p][1] : PARTS[p][1] + PARTS[p][2]]
 
-    def part_parts(p, lead):
+    def block_parts(p):
         cols = pl.ds(PARTS[p][1], PARTS[p][2])
-        if lead:
-            return tuple((lambda ref, k, i=i: ref.at[k, pl.ds(i, 2), :, cols]) for i in (0, 2))
-        return tuple((lambda ref, k, r=r: ref.at[k, pl.ds(*r), cols]) for r in ((0, 48), (48, 32)))
+        return tuple((lambda ref, k, i=i: ref.at[k, pl.ds(i, 2), :, cols]) for i in (0, 2))
 
     def far_ring(p, h):
         m = PARTS[p][0]
-        return raws[h].at[m], x_recv.at[m, h], part_parts(p, True), far[h][1], far[h][3]
-
-    def near_ring(p, h):
-        m = PARTS[p][0]
-        return b_send.at[m, h], b_recv.at[m, h], part_parts(p, False), near[h][1], near[h][3]
+        return raws[h].at[m], x_recv.at[m, h], block_parts(p), far[h][1], far[h][3]
 
     def far_start(p):
         m, start, width = PARTS[p]
         cols = slice(start, start + width)
-        for j, slot in ((2, 0), (1, 1), (3, 2)):
+
+        def away(k):
             for h in range(2):
-                for k in range(4):
+                for j, slot in ((2, 0), (1, 1), (3, 2)):
                     raws[h][m, slot, k, :, cols] = grad_rows(p, h, j, k).astype(BF)
+
+        def mine(k):
+            for h in range(2):
+                grad_own[m, h, k, :, cols] = grad_rows(p, h, 0, k)
+
+        each(4, away)
         out = [ring_start(*far_ring(p, h)) for h in range(2)]
-        for h in range(2):
-            for k in range(4):
-                grad_own[m, h, k, :, cols] = grad_rows(p, h, 0, k)
+        each(4, mine)
         return out
 
     def far_add(p, d):
@@ -583,37 +620,41 @@
         out = []
         for h in range(2):
             ring_wait(d[h])
-            for k in (2, 1, 3, 0):
-                total = (
+
+            def total(k):
+                return (
                     grad_own[m, h, k, :, cols]
                     + x_recv[m, h, 1, k, :, cols].astype(F32)
                     + x_recv[m, h, 2, k, :, cols].astype(F32)
                 )
-                if k == 0:
-                    grad_own[m, h, 0, :, cols] = total
-                else:
-                    b_send[m, h, {2: 0, 1: 1, 3: 2}[k], :, cols] = total.astype(BF)
-            out.append(ring_start(*near_ring(p, h)))
+
+            def away(k):
+                b_send[m, h, k, :, cols] = total(k + 1).astype(BF)
+
+            each(3, away)
+            send, recv = b_send.at[m, h], b_recv.at[m, h]
+            part = pl.ds(start, width)
+            out += [
+                push(send.at[k, :, part], recv.at[k, :, part], near[h][k + 1]) for k in (1, 0, 2)
+            ]
+            grad_own[m, h, 0, :, cols] = total(0)
         return out
-
-    def near_add(p, d):
-        for h in range(2):
-            ring_add(*near_ring(p, h), add_rows, d[h])
 
     def out_cols(owner, start, width):
         return pl.ds(pl.multiple_of(owner * SLICE + start, 128), width)
 
-    out_copies = []
-
     def update(p, d):
         m, start, width = PARTS[p]
-        cols = slice(start, start + width)
-        for h in range(2):
-            ring_wait(d[h])
+        for copy in d:
+            copy.wait_recv()
+
+        def columns(n, h):
+            cols = pl.ds(pl.multiple_of(start + n * 128, 128), 128)
             rows = slice(0, 80) if h == 0 else slice(80, BLOCK)
             high = 80 if h == 0 else 72
             grads = (
                 grad_own[m, h, 0, 0:high, cols]
+                + b_recv[m, h, 0, 0:high, cols].astype(F32)
                 + b_recv[m, h, 1, 0:high, cols].astype(F32)
                 + b_recv[m, h, 2, 0:high, cols].astype(F32)
             )
@@ -628,6 +669,9 @@
             m2[m, rows, cols] = new_second
             par[m, rows, cols] = new_weights
             land[m, 0, rows, cols] = new_weights.astype(BF)
+
+        for h in range(2):
+            each(width // 128, functools.partial(columns, h=h))
         mine = land.at[m, 0, :, pl.ds(start, width)]
 
         def slot(j, k):
@@ -638,18 +682,20 @@
             "right": push(mine, slot(1, 0), y_minus),
             "sib0": push(mine, slot(0, 1), sibling),
         }
+        if p == 3:
+            d["across"] = push(mine, slot(2, 0), y_ring[2])
         out_store(p, 0, 0)
         if p in (1, 3):
-            out_copies.append(move(m1.at[m], o_m1.at[m]))
-            out_copies.append(move(m2.at[m], o_m2.at[m]))
-            out_copies.append(move(par.at[m], o_par.at[m]))
+            move(m1.at[m], o_m1.at[m])
+            move(m2.at[m], o_m2.at[m])
+            move(par.at[m], o_par.at[m])
         return d
 
     def out_store(p, j, k):
         m, start, width = PARTS[p]
         owner = turn(y, j) * 2 + (c if k == 0 else 1 - c)
         block = land.at[m, 2 * j + k, :, pl.ds(start, width)]
-        out_copies.append(move(block, o_roll.at[m, :, out_cols(owner, start, width)]))
+        move(block, o_roll.at[m, :, out_cols(owner, start, width)])
 
     def out_on(p, d):
         m, start, width = PARTS[p]
@@ -660,7 +706,8 @@
         ):
             d[key].wait_recv()
             cols = pl.ds(at_, wide)
-            d[key, "across"] = push(land.at[m, 2 * j, :, cols], land.at[m, 4, :, cols], to)
+            if p != 3:
+                d[key, "across"] = push(land.at[m, 2 * j, :, cols], land.at[m, 4, :, cols], to)
             cols = pl.ds(start, width)
             d[key, "sib"] = push(
                 land.at[m, 2 * j, :, cols], land.at[m, 2 * j + 1, :, cols], sibling
@@ -669,8 +716,8 @@
 
     def out_end(p, d):
         m, start, width = PARTS[p]
-        d["left", "across"].wait_recv()
-        d["right", "across"].wait_recv()
+        for key in (("across",) if p == 3 else (("left", "across"), ("right", "across"))):
+            d[key].wait_recv()
         cols = pl.ds(start, width)
         d["sib2"] = push(land.at[m, 4, :, cols], land.at[m, 5, :, cols], sibling)
         out_store(p, 2, 0)
@@ -686,13 +733,13 @@
         out_store(p, 2, 1)
 
     for copy in weights_sent:
-        copy.wait_send()
+        copy.wait()
     grad[pl.ds(D, 8), :] = jnp.zeros((8, SLICE), F32)
 
-    for n, (start, width) in enumerate(TILES):
-        for p in (0, 1):
-            cols = slice(PARTS[p][1], PARTS[p][1] + PARTS[p][2])
-            grad[start : start + width, cols] = grad_part(p, bk, 0, n)
+    def first_rows(at_, wide):
+        grad[pl.ds(at_, wide), :] = grad_part(bk, 0, at_, wide, 0, SLICE)
+
+    over_width(first_rows)
     gather_on(bk, 1, back1)
     back_pre(0)
     gather_near(bk, 1, back1)
@@ -700,14 +747,23 @@
     gather_sib(back1)
 
     def down_part(p):
-        cols = slice(PARTS[p][1], PARTS[p][1] + PARTS[p][2])
-        for n, (start, width) in enumerate(TILES):
-            grad[start : start + width, cols] += grad_part(p, bk, 1, n)
+        start, width = PARTS[p][1:]
+
+        def body(at_, wide):
+            cols = slice(start, start + width)
+            grad[pl.ds(at_, wide), cols] += grad_part(bk, 1, at_, wide, start, width)
+
+        over_width(body)
 
     def up_part(p):
-        cols = slice(PARTS[p][1], PARTS[p][1] + PARTS[p][2])
-        for n, (start, width) in enumerate(TILES):
-            grad[start : start + width, cols] = grad_part(p, hid, 0, n) + grad_part(p, hid, 1, n)
+        start, width = PARTS[p][1:]
+
+        def body(at_, wide):
+            grad[pl.ds(at_, wide), start : start + width] = grad_part(
+                hid, 0, at_, wide, start, width
+            ) + grad_part(hid, 1, at_, wide, start, width)
+
+        over_width(body)
 
     down_part(0)
     far0 = far_start(0)
@@ -725,44 +781,40 @@
     near1 = near_start(1, far1)
     far3 = far_start(3)
     far_add(2, far2)
-    near_add(0, near0)
-    near_add(1, near1)
+    out0 = update(0, near0)
+    out1 = update(1, near1)
     far_add(3, far3)
-    out0 = update(0, near0)
     near2 = near_start(2, far2)
-    out1 = update(1, near1)
+    out_on(0, out0)
+    out_on(1, out1)
     near3 = near_start(3, far3)
-    near_add(2, near2)
-    near_add(3, near3)
-    out_on(0, out0)
     out2 = update(2, near2)
+    out_end(0, out0)
+    out_end(1, out1)
     out3 = update(3, near3)
-    out_on(1, out1)
-    out_end(0, out0)
     out_on(2, out2)
-    out_end(1, out1)
     out_on(3, out3)
     out_end(2, out2)
     out_end(3, out3)
     for p, out in enumerate((out0, out1, out2, out3)):
         out_sib(p, out)
-    for copy in out_copies:
+    assert fresh_id[0] <= N_RECV, fresh_id[0]
+    for copy in moves + sends:
         copy.wait()
-    for copy in sent:
-        copy.wait_send()
 
 
 def settle(*refs):
     sources, targets, held, sem = refs[:4], refs[4:8], refs[8:12], refs[12]
-    pieces = [(i, m) for i in range(4) for m in range(2)]
-    reads = []
+    pieces = [(i, m) for i in (3, 0, 1, 2) for m in range(2)]
+    reads, writes = [], []
     for n, (i, m) in enumerate(pieces):
-        reads.append(pltpu.make_async_copy(sources[i].at[m], held[i].at[m], sem.at[n]))
+        there, here = sources[i].at[m], held[i].at[m]
+        reads.append(pltpu.make_async_copy(there, here, sem.at[n]))
         reads[-1].start()
-    writes = []
     for n, (i, m) in enumerate(pieces):
         reads[n].wait()
-        writes.append(pltpu.make_async_copy(held[i].at[m], targets[i].at[m], sem.at[8 + n]))
+        here, there = held[i].at[m], targets[i].at[m]
+        writes.append(pltpu.make_async_copy(here, there, sem.at[len(pieces) + n]))
         writes[-1].start()
     for write in writes:
         write.wait()
@@ -824,9 +876,9 @@
             pltpu.SMEM((2,), F32),
             pltpu.VMEM((2, PATCH), jnp.int32),
             pltpu.VMEM((3, 2, D), F32),
-            pltpu.SemaphoreType.DMA((N_COPIES,)),
-            pltpu.SemaphoreType.DMA((N_COPIES,)),
-            pltpu.SemaphoreType.DMA((56,)),
+            pltpu.SemaphoreType.DMA((N_SEND + N_PAIR,)),
+            pltpu.SemaphoreType.DMA((N_RECV + N_PAIR,)),
+            pltpu.SemaphoreType.DMA((N_LOCAL,)),
         ],
         compiler_params=pltpu.CompilerParams(
             collective_id=0, has_side_effects=True, vmem_limit_bytes=63 << 20

time: 169 us -> 162 us (0.959)
  Pallas kernels: 168 us -> 161 us
    pallas_call x1, Pallas kernels: 163 us -> 157 us  [per_device(): pl.pallas_call(kernel, out_shape=(shard, shard, shard, jax.ShapeDtypeStru...]
where the time goes in v3:
time: 162 us; the launch traced here: 161 us
  Pallas kernels  161 us (99%)
    pallas_call x1, Pallas kernels, per_device(): pl.pallas_call(kernel, out_shape=(shard, shard, shard, jax.ShapeDtypeStru...  157 us
    pallas_call x1, Pallas kernels, per_device(): pl.pallas_call(settle, out_shape=tuple((jax.ShapeDtypeStruct(o.shape, o.d...  3.95 us

profile of v3, /device:TPU:1, one launch (start us, length us, event | category | flops | bytes accessed | tf_op | source)
XLA Modules:
  0.0 161.4 jit_solution(15318743326242694018)
XLA Ops:
  0.6 156.6 %shard_map.156 = (f32[2,152,640]{2,1,0:T(8,128)}, f32[2,152,640]{2,1,0:T(8,128)}, f32[2,152,640]{2,1,0:T(8,128)}, bf16[2,152,5120]{2,1,0:T(8,128)(2,1)}) custom-call(f32[2]{0:T(128)} %rewards_h.1, s32[2]{0:T(128)} %group_ids_h.1, s32[2]{0:T(128)} %step_index_h.1, s32[2]{0:T(128)} %valid_steps_h.1, f32[2]{0:T(128)} %step_ratio_h.1, s32[2,80]{1,0:T(2,128)} %mask_h.1, ...), custom_call_target="tpu_custom_call" | custom-call | tf_op jit(solution)/shard_map/pallas_call | solution.py:840
  157.3 3.9 %shard_map.157 = (f32[2,152,640]{2,1,0:T(8,128)}, f32[2,152,640]{2,1,0:T(8,128)}, f32[2,152,640]{2,1,0:T(8,128)}, bf16[2,152,5120]{2,1,0:T(8,128)(2,1)}) custom-call(f32[2,152,640]{2,1,0:T(8,128)} %get-tuple-element.8.refs_0_, f32[2,152,640]{2,1,0:T(8,128)} %get-tuple-element.9.refs_1_, f32[2,152,640]{2,1,0:T(8,128)} %get-tuple-element.10.refs_2_, ...), custom_call_target="tpu_custom_call" | custom-call | tf_op jit(solution)/shard_map/pallas_call | solution.py:902

commit v4 on v3

--- a/solution.py
+++ b/solution.py
@@ -34,7 +34,7 @@
 FIRST = (((0,), (0,)), ((), ()))
 N_SEND = 48
 N_PAIR = 8
-N_RECV = 141
+N_RECV = 167
 N_LOCAL = 20
 
 
@@ -423,16 +423,15 @@
         value = lax.dot_general(act[s, i], asm_down[cols, :], LAST, preferred_element_type=F32)
         return cols, value
 
-    def branch_away(s):
-        def body(n):
+    def branch_half(s, half):
+        def away(q):
+            n = 2 * half + q
             value = branch_tile(s, 1, n)[1]
             asm_up[pl.ds(pl.multiple_of((s * 4 + n) * 320, CHUNK), 320), :] = value.astype(BF)
             pair_copy(s, n).start()
 
-        each(4, body)
-
-    def branch_mine(s):
-        def body(n):
+        def mine(q):
+            n = 2 * half + q
             cols, value = branch_tile(s, 0, n)
             pair_copy(s, n).wait()
             value = value + sib_recv[s, n].astype(F32)
@@ -440,7 +439,8 @@
             for j, k in ((2, 0), (1, 1), (3, 2)):
                 y_send[s, k, :, cols] = value[j * 80 : j * 80 + 80].astype(BF)
 
-        each(4, body)
+        each(2, away)
+        each(2, mine)
 
     def ring_start(send, recv, parts, plus, minus):
         lo, hi = parts
@@ -478,11 +478,23 @@
 
     col_parts = tuple((lambda ref, k, cols=cols: ref.at[k, :, cols]) for cols in COLS)
 
-    def branch_ring(s):
-        return ring_start(y_send.at[s], y_recv.at[s], col_parts, y_plus, y_minus)
-
-    def branch_add(s, d):
-        ring_add(y_send.at[s], y_recv.at[s], col_parts, y_plus, y_minus, add_rows, d)
+    def branch_push(s, half, d):
+        lo, hi = col_parts
+        send, recv = y_send.at[s], y_recv.at[s]
+        if half == 1:
+            d["across_hi"] = push(hi(send, 0), hi(recv, 0), y_plus)
+            d["minus_hi"] = push(hi(send, 2), hi(recv, 2), y_minus)
+        else:
+            d["across_lo"] = push(lo(send, 0), lo(recv, 0), y_minus)
+            d["plus_lo"] = push(lo(send, 1), lo(recv, 1), y_plus)
+
+    def branch_add(s, half, d):
+        part = col_parts[half]
+        send, recv = y_send.at[s], y_recv.at[s]
+        key, k, to = (("lo", 2, y_minus), ("hi", 1, y_plus))[half]
+        d["across_" + key].wait_recv()
+        add_rows(part(send, k), part(recv, 0))
+        d[("minus_lo", "plus_hi")[half]] = push(part(send, k), part(recv, k), to)
 
     def back_rows(s, d):
         ring_wait(d)
@@ -524,9 +536,11 @@
 
         lax.fori_loop(0, PATCH // CHUNK, back_body, 0)
 
-    branch_away(0)
-    branch_mine(0)
-    ring0 = branch_ring(0)
+    ring0, ring1 = {}, {}
+    branch_half(0, 1)
+    branch_push(0, 1, ring0)
+    branch_half(0, 0)
+    branch_push(0, 0, ring0)
     stats_sum(2, stats_copies)
     stats_copies = stats_send(3)
 
@@ -540,15 +554,18 @@
         mask_col[s] = jnp.broadcast_to(column, (PATCH, 128))
         npatch.append(jnp.maximum(jnp.sum(column, axis=0, keepdims=True), 1.0))
 
-    branch_away(1)
-    branch_mine(1)
-    branch_add(0, ring0)
-    ring1 = branch_ring(1)
+    branch_half(1, 1)
+    branch_push(1, 1, ring1)
+    branch_add(0, 1, ring0)
+    branch_half(1, 0)
+    branch_push(1, 0, ring1)
+    branch_add(0, 0, ring0)
     stats_sum(3, stats_copies)
     stale_in.wait()
     noise_in.wait()
+    branch_add(1, 1, ring1)
+    branch_add(1, 0, ring1)
     back_rows(0, ring0)
-    branch_add(1, ring1)
     stage[0] = 2
     back0 = gather_own(bk, 0)
     back_rows(1, ring1)
@@ -567,7 +584,8 @@
 
         lax.fori_loop(0, 2, body, 0)
 
-    PARTS = ((1, 0, 256), (1, 256, 384), (0, 0, 384), (0, 384, 256))
+    PARTS = ((1, 0, 256), (1, 256, 384), (0, 0, 256), (0, 256, 256), (0, 512, 128))
+    final = len(PARTS) - 1
 
     def over_width(body):
         each(3, lambda n: body(pl.multiple_of(n * SLICE, 128), SLICE))
@@ -682,10 +700,10 @@
             "right": push(mine, slot(1, 0), y_minus),
             "sib0": push(mine, slot(0, 1), sibling),
         }
-        if p == 3:
+        if p == final:
             d["across"] = push(mine, slot(2, 0), y_ring[2])
         out_store(p, 0, 0)
-        if p in (1, 3):
+        if p in (1, final):
             move(m1.at[m], o_m1.at[m])
             move(m2.at[m], o_m2.at[m])
             move(par.at[m], o_par.at[m])
@@ -706,7 +724,7 @@
         ):
             d[key].wait_recv()
             cols = pl.ds(at_, wide)
-            if p != 3:
+            if p != final:
                 d[key, "across"] = push(land.at[m, 2 * j, :, cols], land.at[m, 4, :, cols], to)
             cols = pl.ds(start, width)
             d[key, "sib"] = push(
@@ -716,7 +734,7 @@
 
     def out_end(p, d):
         m, start, width = PARTS[p]
-        for key in (("across",) if p == 3 else (("left", "across"), ("right", "across"))):
+        for key in (("across",) if p == final else (("left", "across"), ("right", "across"))):
             d[key].wait_recv()
         cols = pl.ds(start, width)
         d["sib2"] = push(land.at[m, 4, :, cols], land.at[m, 5, :, cols], sibling)
@@ -775,28 +793,35 @@
     far_add(1, far1)
     far2 = far_start(2)
     up_part(3)
+    far3 = far_start(3)
+    up_part(4)
+    far4 = far_start(4)
+    near0 = near_start(0, far0)
+    near1 = near_start(1, far1)
+    far_add(2, far2)
     m1_in.wait()
     m2_in.wait()
-    near0 = near_start(0, far0)
-    near1 = near_start(1, far1)
-    far3 = far_start(3)
-    far_add(2, far2)
+    far_add(3, far3)
+    far_add(4, far4)
     out0 = update(0, near0)
     out1 = update(1, near1)
-    far_add(3, far3)
     near2 = near_start(2, far2)
+    near3 = near_start(3, far3)
     out_on(0, out0)
+    near4 = near_start(4, far4)
+    out2 = update(2, near2)
     out_on(1, out1)
-    near3 = near_start(3, far3)
-    out2 = update(2, near2)
+    out3 = update(3, near3)
     out_end(0, out0)
+    out4 = update(4, near4)
     out_end(1, out1)
-    out3 = update(3, near3)
     out_on(2, out2)
     out_on(3, out3)
     out_end(2, out2)
+    out_on(4, out4)
     out_end(3, out3)
-    for p, out in enumerate((out0, out1, out2, out3)):
+    out_end(4, out4)
+    for p, out in enumerate((out0, out1, out2, out3, out4)):
         out_sib(p, out)
     assert fresh_id[0] <= N_RECV, fresh_id[0]
     for copy in moves + sends:

time: 162 us -> 159 us (0.981)
  Pallas kernels: 161 us -> 159 us
    pallas_call x1, Pallas kernels: 157 us -> 155 us  [per_device(): pl.pallas_call(kernel, out_shape=(shard, shard, shard, jax.ShapeDtypeStru...]
where the time goes in v4:
time: 159 us
  Pallas kernels  159 us (100%)
    pallas_call x1, Pallas kernels, per_device(): pl.pallas_call(kernel, out_shape=(shard, shard, shard, jax.ShapeDtypeStru...  155 us
    pallas_call x1, Pallas kernels, per_device(): pl.pallas_call(settle, out_shape=tuple((jax.ShapeDtypeStruct(o.shape, o.d...  3.95 us

profile of v4, /device:TPU:1, one launch (start us, length us, event | category | flops | bytes accessed | tf_op | source)
XLA Modules:
  0.0 159.3 jit_solution(16159995520291289458)
XLA Ops:
  0.6 154.6 %shard_map.156 = (f32[2,152,640]{2,1,0:T(8,128)}, f32[2,152,640]{2,1,0:T(8,128)}, f32[2,152,640]{2,1,0:T(8,128)}, bf16[2,152,5120]{2,1,0:T(8,128)(2,1)}) custom-call(f32[2]{0:T(128)} %rewards_h.1, s32[2]{0:T(128)} %group_ids_h.1, s32[2]{0:T(128)} %step_index_h.1, s32[2]{0:T(128)} %valid_steps_h.1, f32[2]{0:T(128)} %step_ratio_h.1, s32[2,80]{1,0:T(2,128)} %mask_h.1, ...), custom_call_target="tpu_custom_call" | custom-call | tf_op jit(solution)/shard_map/pallas_call | solution.py:865
  155.2 3.9 %shard_map.157 = (f32[2,152,640]{2,1,0:T(8,128)}, f32[2,152,640]{2,1,0:T(8,128)}, f32[2,152,640]{2,1,0:T(8,128)}, bf16[2,152,5120]{2,1,0:T(8,128)(2,1)}) custom-call(f32[2,152,640]{2,1,0:T(8,128)} %get-tuple-element.8.refs_0_, f32[2,152,640]{2,1,0:T(8,128)} %get-tuple-element.9.refs_1_, f32[2,152,640]{2,1,0:T(8,128)} %get-tuple-element.10.refs_2_, ...), custom_call_target="tpu_custom_call" | custom-call | tf_op jit(solution)/shard_map/pallas_call | solution.py:927

commit v5 on v4

--- a/solution.py
+++ b/solution.py
@@ -703,11 +703,12 @@
         if p == final:
             d["across"] = push(mine, slot(2, 0), y_ring[2])
         out_store(p, 0, 0)
-        if p in (1, final):
-            move(m1.at[m], o_m1.at[m])
-            move(m2.at[m], o_m2.at[m])
-            move(par.at[m], o_par.at[m])
         return d
+
+    def state_store(m):
+        move(m1.at[m], o_m1.at[m])
+        move(m2.at[m], o_m2.at[m])
+        move(par.at[m], o_par.at[m])
 
     def out_store(p, j, k):
         m, start, width = PARTS[p]
@@ -761,15 +762,33 @@
     gather_on(bk, 1, back1)
     back_pre(0)
     gather_near(bk, 1, back1)
+    for j in (0, 1, 3):
+        back1["sib%d" % j].wait_recv()
+
+    def grad_blocks(at_, wide, blocks, start, width):
+        left = bk[1, :, blocks, :, pl.ds(at_, wide)]
+        n = left.shape[1] * PATCH
+        first_row = blocks.start * PATCH
+        right = act[1, :, first_row : first_row + n, start : start + width].reshape(2 * n, width)
+        return lax.dot_general(
+            left.reshape(2 * n, wide), right, FIRST, preferred_element_type=F32
+        )
+
+    def early_rows(at_, wide):
+        grad[pl.ds(at_, wide), :] += grad_blocks(at_, wide, slice(0, 2), 0, SLICE) + grad_blocks(
+            at_, wide, slice(3, 4), 0, SLICE
+        )
+
+    over_width(early_rows)
     gather_end(bk, 1, back1)
-    gather_sib(back1)
+    back1["sib2"].wait_recv()
 
     def down_part(p):
         start, width = PARTS[p][1:]
 
         def body(at_, wide):
             cols = slice(start, start + width)
-            grad[pl.ds(at_, wide), cols] += grad_part(bk, 1, at_, wide, start, width)
+            grad[pl.ds(at_, wide), cols] += grad_blocks(at_, wide, slice(2, 3), start, width)
 
         over_width(body)
 
@@ -788,38 +807,40 @@
     down_part(1)
     far1 = far_start(1)
     back_pre(1)
+    far_add(1, far1)
     far_add(0, far0)
     up_part(2)
-    far_add(1, far1)
     far2 = far_start(2)
+    near1 = near_start(1, far1)
     up_part(3)
+    far_add(2, far2)
     far3 = far_start(3)
-    up_part(4)
-    far4 = far_start(4)
     near0 = near_start(0, far0)
-    near1 = near_start(1, far1)
-    far_add(2, far2)
     m1_in.wait()
     m2_in.wait()
+    out1 = update(1, near1)
     far_add(3, far3)
+    up_part(4)
+    near2 = near_start(2, far2)
+    far4 = far_start(4)
+    out0 = update(0, near0)
+    state_store(1)
+    out_on(1, out1)
+    near3 = near_start(3, far3)
     far_add(4, far4)
-    out0 = update(0, near0)
-    out1 = update(1, near1)
-    near2 = near_start(2, far2)
-    near3 = near_start(3, far3)
+    out2 = update(2, near2)
+    out3 = update(3, near3)
+    near4 = near_start(4, far4)
+    out_on(2, out2)
     out_on(0, out0)
-    near4 = near_start(4, far4)
-    out2 = update(2, near2)
-    out_on(1, out1)
-    out3 = update(3, near3)
+    out_on(3, out3)
+    out4 = update(4, near4)
+    state_store(0)
     out_end(0, out0)
-    out4 = update(4, near4)
+    out_end(3, out3)
     out_end(1, out1)
-    out_on(2, out2)
-    out_on(3, out3)
+    out_on(4, out4)
     out_end(2, out2)
-    out_on(4, out4)
-    out_end(3, out3)
     out_end(4, out4)
     for p, out in enumerate((out0, out1, out2, out3, out4)):
         out_sib(p, out)

time: 159 us -> 160 us (level)
  no operation moved by 1% of the time
where the time goes in v5:
time: 160 us
  Pallas kernels  159 us (99%)
    pallas_call x1, Pallas kernels, per_device(): pl.pallas_call(kernel, out_shape=(shard, shard, shard, jax.ShapeDtypeStru...  155 us
    pallas_call x1, Pallas kernels, per_device(): pl.pallas_call(settle, out_shape=tuple((jax.ShapeDtypeStruct(o.shape, o.d...  3.95 us

profile of v5, /device:TPU:1, one launch (start us, length us, event | category | flops | bytes accessed | tf_op | source)
XLA Modules:
  0.0 159.5 jit_solution(11831616204698852961)
XLA Ops:
  0.6 154.8 %shard_map.156 = (f32[2,152,640]{2,1,0:T(8,128)}, f32[2,152,640]{2,1,0:T(8,128)}, f32[2,152,640]{2,1,0:T(8,128)}, bf16[2,152,5120]{2,1,0:T(8,128)(2,1)}) custom-call(f32[2]{0:T(128)} %rewards_h.1, s32[2]{0:T(128)} %group_ids_h.1, s32[2]{0:T(128)} %step_index_h.1, s32[2]{0:T(128)} %valid_steps_h.1, f32[2]{0:T(128)} %step_ratio_h.1, s32[2,80]{1,0:T(2,128)} %mask_h.1, ...), custom_call_target="tpu_custom_call" | custom-call | tf_op jit(solution)/shard_map/pallas_call | solution.py:886
  155.4 3.9 %shard_map.157 = (f32[2,152,640]{2,1,0:T(8,128)}, f32[2,152,640]{2,1,0:T(8,128)}, f32[2,152,640]{2,1,0:T(8,128)}, bf16[2,152,5120]{2,1,0:T(8,128)(2,1)}) custom-call(f32[2,152,640]{2,1,0:T(8,128)} %get-tuple-element.8.refs_0_, f32[2,152,640]{2,1,0:T(8,128)} %get-tuple-element.9.refs_1_, f32[2,152,640]{2,1,0:T(8,128)} %get-tuple-element.10.refs_2_, ...), custom_call_target="tpu_custom_call" | custom-call | tf_op jit(solution)/shard_map/pallas_call | solution.py:948

commit v6 on v5

--- a/solution.py
+++ b/solution.py
@@ -32,10 +32,10 @@
 OUT_COLS = ((0, 384), (384, 256))
 LAST = (((1,), (1,)), ((), ()))
 FIRST = (((0,), (0,)), ((), ()))
-N_SEND = 48
+N_SEND = 40
 N_PAIR = 8
 N_RECV = 167
-N_LOCAL = 20
+N_LOCAL = 16
 
 
 def gelu_parts(pre):
@@ -692,29 +692,26 @@
             each(width // 128, functools.partial(columns, h=h))
         mine = land.at[m, 0, :, pl.ds(start, width)]
 
-        def slot(j, k):
-            return land.at[m, 2 * j + k, :, pl.ds(start, width)]
-
-        d = {
-            "left": push(mine, slot(3, 0), y_plus),
-            "right": push(mine, slot(1, 0), y_minus),
-            "sib0": push(mine, slot(0, 1), sibling),
-        }
+        def slot(j):
+            return land.at[m, j, :, pl.ds(start, width)]
+
+        d = {"left": push(mine, slot(3), y_plus), "right": push(mine, slot(1), y_minus)}
         if p == final:
-            d["across"] = push(mine, slot(2, 0), y_ring[2])
-        out_store(p, 0, 0)
+            d["across"] = push(mine, slot(2), y_ring[2])
+        d["sib0"] = out_give(p, 0)
+        for state, result in ((m1, o_m1), (m2, o_m2), (par, o_par)):
+            part = pl.ds(start, width)
+            move(state.at[m, :, part], result.at[m, :, part])
         return d
 
-    def state_store(m):
-        move(m1.at[m], o_m1.at[m])
-        move(m2.at[m], o_m2.at[m])
-        move(par.at[m], o_par.at[m])
-
-    def out_store(p, j, k):
+    def out_give(p, j):
         m, start, width = PARTS[p]
-        owner = turn(y, j) * 2 + (c if k == 0 else 1 - c)
-        block = land.at[m, 2 * j + k, :, pl.ds(start, width)]
-        move(block, o_roll.at[m, :, out_cols(owner, start, width)])
+        block = land.at[m, j, :, pl.ds(start, width)]
+        owner = turn(y, j) * 2
+        place = o_roll.at[m, :, out_cols(owner + c, start, width)]
+        copy = push(block, place, sibling, o_roll.at[m, :, out_cols(owner + 1 - c, start, width)])
+        move(block, place)
+        return copy
 
     def out_on(p, d):
         m, start, width = PARTS[p]
@@ -726,30 +723,17 @@
             d[key].wait_recv()
             cols = pl.ds(at_, wide)
             if p != final:
-                d[key, "across"] = push(land.at[m, 2 * j, :, cols], land.at[m, 4, :, cols], to)
-            cols = pl.ds(start, width)
-            d[key, "sib"] = push(
-                land.at[m, 2 * j, :, cols], land.at[m, 2 * j + 1, :, cols], sibling
-            )
-            out_store(p, j, 0)
+                d[key, "across"] = push(land.at[m, j, :, cols], land.at[m, 2, :, cols], to)
+            d[key, "sib"] = out_give(p, j)
 
     def out_end(p, d):
-        m, start, width = PARTS[p]
         for key in (("across",) if p == final else (("left", "across"), ("right", "across"))):
             d[key].wait_recv()
-        cols = pl.ds(start, width)
-        d["sib2"] = push(land.at[m, 4, :, cols], land.at[m, 5, :, cols], sibling)
-        out_store(p, 2, 0)
-
-    def out_sib(p, d):
-        d["sib0"].wait_recv()
-        out_store(p, 0, 1)
-        d["left", "sib"].wait_recv()
-        out_store(p, 3, 1)
-        d["right", "sib"].wait_recv()
-        out_store(p, 1, 1)
-        d["sib2"].wait_recv()
-        out_store(p, 2, 1)
+        d["sib2"] = out_give(p, 2)
+
+    def out_sib(d):
+        for key in ("sib0", ("left", "sib"), ("right", "sib"), "sib2"):
+            d[key].wait_recv()
 
     for copy in weights_sent:
         copy.wait()
@@ -824,7 +808,6 @@
     near2 = near_start(2, far2)
     far4 = far_start(4)
     out0 = update(0, near0)
-    state_store(1)
     out_on(1, out1)
     near3 = near_start(3, far3)
     far_add(4, far4)
@@ -835,15 +818,14 @@
     out_on(0, out0)
     out_on(3, out3)
     out4 = update(4, near4)
-    state_store(0)
     out_end(0, out0)
     out_end(3, out3)
     out_end(1, out1)
     out_on(4, out4)
     out_end(2, out2)
     out_end(4, out4)
-    for p, out in enumerate((out0, out1, out2, out3, out4)):
-        out_sib(p, out)
+    for out in (out0, out1, out2, out3, out4):
+        out_sib(out)
     assert fresh_id[0] <= N_RECV, fresh_id[0]
     for copy in moves + sends:
         copy.wait()
@@ -911,7 +893,7 @@
             pltpu.VMEM((2, BLOCK, SLICE), F32),
             pltpu.VMEM((2, BLOCK, SLICE), F32),
             pltpu.VMEM((2, BLOCK, SLICE), F32),
-            pltpu.VMEM((2, 8, BLOCK, SLICE), BF),
+            pltpu.VMEM((2, 4, BLOCK, SLICE), BF),
             pltpu.VMEM((2, PATCH, 128), F32),
             pltpu.VMEM((8, 128), F32),
             pltpu.VMEM((4, 4, 8, 128), F32),

time: 160 us -> 159 us (level)
  no operation moved by 1% of the time
where the time goes in v6:
time: 159 us
  Pallas kernels  158 us (99%)
    pallas_call x1, Pallas kernels, per_device(): pl.pallas_call(kernel, out_shape=(shard, shard, shard, jax.ShapeDtypeStru...  154 us
    pallas_call x1, Pallas kernels, per_device(): pl.pallas_call(settle, out_shape=tuple((jax.ShapeDtypeStruct(o.shape, o.d...  3.95 us

profile of v6, /device:TPU:1, one launch (start us, length us, event | category | flops | bytes accessed | tf_op | source)
XLA Modules:
  0.0 158.7 jit_solution(2653756998990030953)
XLA Ops:
  0.6 154.0 %shard_map.156 = (f32[2,152,640]{2,1,0:T(8,128)}, f32[2,152,640]{2,1,0:T(8,128)}, f32[2,152,640]{2,1,0:T(8,128)}, bf16[2,152,5120]{2,1,0:T(8,128)(2,1)}) custom-call(f32[2]{0:T(128)} %rewards_h.1, s32[2]{0:T(128)} %group_ids_h.1, s32[2]{0:T(128)} %step_index_h.1, s32[2]{0:T(128)} %valid_steps_h.1, f32[2]{0:T(128)} %step_ratio_h.1, s32[2,80]{1,0:T(2,128)} %mask_h.1, ...), custom_call_target="tpu_custom_call" | custom-call | tf_op jit(solution)/shard_map/pallas_call | solution.py:868
  154.6 3.9 %shard_map.157 = (f32[2,152,640]{2,1,0:T(8,128)}, f32[2,152,640]{2,1,0:T(8,128)}, f32[2,152,640]{2,1,0:T(8,128)}, bf16[2,152,5120]{2,1,0:T(8,128)(2,1)}) custom-call(f32[2,152,640]{2,1,0:T(8,128)} %get-tuple-element.8.refs_0_, f32[2,152,640]{2,1,0:T(8,128)} %get-tuple-element.9.refs_1_, f32[2,152,640]{2,1,0:T(8,128)} %get-tuple-element.10.refs_2_, ...), custom_call_target="tpu_custom_call" | custom-call | tf_op jit(solution)/shard_map/pallas_call | solution.py:930

commit v7 on v6

--- a/solution.py
+++ b/solution.py
@@ -200,12 +200,12 @@
             [par[m, 144:BLOCK, :], jnp.zeros((8, SLICE), F32)], axis=0
         ).astype(BF)
 
-    def each(n, body):
+    def each(n, body, unroll=1):
         def step(i, carry):
             body(i)
             return carry
 
-        lax.fori_loop(0, n, step, 0)
+        lax.fori_loop(0, n, step, 0, unroll=unroll)
 
     def modulated(s):
         shift = mod[0, s : s + 1, :]
@@ -439,8 +439,8 @@
             for j, k in ((2, 0), (1, 1), (3, 2)):
                 y_send[s, k, :, cols] = value[j * 80 : j * 80 + 80].astype(BF)
 
-        each(2, away)
-        each(2, mine)
+        each(2, away, unroll=2)
+        each(2, mine, unroll=2)
 
     def ring_start(send, recv, parts, plus, minus):
         lo, hi = parts
@@ -585,7 +585,7 @@
         lax.fori_loop(0, 2, body, 0)
 
     PARTS = ((1, 0, 256), (1, 256, 384), (0, 0, 256), (0, 256, 256), (0, 512, 128))
-    final = len(PARTS) - 1
+    DIRECT = (3, 4)
 
     def over_width(body):
         each(3, lambda n: body(pl.multiple_of(n * SLICE, 128), SLICE))
@@ -696,7 +696,7 @@
             return land.at[m, j, :, pl.ds(start, width)]
 
         d = {"left": push(mine, slot(3), y_plus), "right": push(mine, slot(1), y_minus)}
-        if p == final:
+        if p in DIRECT:
             d["across"] = push(mine, slot(2), y_ring[2])
         d["sib0"] = out_give(p, 0)
         for state, result in ((m1, o_m1), (m2, o_m2), (par, o_par)):
@@ -722,12 +722,12 @@
         ):
             d[key].wait_recv()
             cols = pl.ds(at_, wide)
-            if p != final:
+            if p not in DIRECT:
                 d[key, "across"] = push(land.at[m, j, :, cols], land.at[m, 2, :, cols], to)
             d[key, "sib"] = out_give(p, j)
 
     def out_end(p, d):
-        for key in (("across",) if p == final else (("left", "across"), ("right", "across"))):
+        for key in (("across",) if p in DIRECT else (("left", "across"), ("right", "across"))):
             d[key].wait_recv()
         d["sib2"] = out_give(p, 2)
 
@@ -791,38 +791,38 @@
     down_part(1)
     far1 = far_start(1)
     back_pre(1)
-    far_add(1, far1)
     far_add(0, far0)
     up_part(2)
+    far_add(1, far1)
+    up_part(3)
     far2 = far_start(2)
     near1 = near_start(1, far1)
-    up_part(3)
     far_add(2, far2)
     far3 = far_start(3)
-    near0 = near_start(0, far0)
+    up_part(4)
     m1_in.wait()
     m2_in.wait()
     out1 = update(1, near1)
+    near2 = near_start(2, far2)
     far_add(3, far3)
-    up_part(4)
-    near2 = near_start(2, far2)
+    near0 = near_start(0, far0)
     far4 = far_start(4)
-    out0 = update(0, near0)
     out_on(1, out1)
+    out2 = update(2, near2)
     near3 = near_start(3, far3)
     far_add(4, far4)
-    out2 = update(2, near2)
+    out0 = update(0, near0)
+    out_on(2, out2)
+    out_end(1, out1)
     out3 = update(3, near3)
     near4 = near_start(4, far4)
-    out_on(2, out2)
     out_on(0, out0)
+    out4 = update(4, near4)
     out_on(3, out3)
-    out4 = update(4, near4)
-    out_end(0, out0)
     out_end(3, out3)
-    out_end(1, out1)
     out_on(4, out4)
     out_end(2, out2)
+    out_end(0, out0)
     out_end(4, out4)
     for out in (out0, out1, out2, out3, out4):
         out_sib(out)

time: 159 us -> 158 us (level)
  no operation moved by 1% of the time
where the time goes in v7:
time: 158 us
  Pallas kernels  157 us (99%)
    pallas_call x1, Pallas kernels, per_device(): pl.pallas_call(kernel, out_shape=(shard, shard, shard, jax.ShapeDtypeStru...  153 us
    pallas_call x1, Pallas kernels, per_device(): pl.pallas_call(settle, out_shape=tuple((jax.ShapeDtypeStruct(o.shape, o.d...  3.95 us

profile of v7, /device:TPU:1, one launch (start us, length us, event | category | flops | bytes accessed | tf_op | source)
XLA Modules:
  0.0 158.2 jit_solution(12765848202524099625)
XLA Ops:
  0.6 153.4 %shard_map.156 = (f32[2,152,640]{2,1,0:T(8,128)}, f32[2,152,640]{2,1,0:T(8,128)}, f32[2,152,640]{2,1,0:T(8,128)}, bf16[2,152,5120]{2,1,0:T(8,128)(2,1)}) custom-call(f32[2]{0:T(128)} %rewards_h.1, s32[2]{0:T(128)} %group_ids_h.1, s32[2]{0:T(128)} %step_index_h.1, s32[2]{0:T(128)} %valid_steps_h.1, f32[2]{0:T(128)} %step_ratio_h.1, s32[2,80]{1,0:T(2,128)} %mask_h.1, ...), custom_call_target="tpu_custom_call" | custom-call | tf_op jit(solution)/shard_map/pallas_call | solution.py:868
  154.0 3.9 %shard_map.157 = (f32[2,152,640]{2,1,0:T(8,128)}, f32[2,152,640]{2,1,0:T(8,128)}, f32[2,152,640]{2,1,0:T(8,128)}, bf16[2,152,5120]{2,1,0:T(8,128)(2,1)}) custom-call(f32[2,152,640]{2,1,0:T(8,128)} %get-tuple-element.8.refs_0_, f32[2,152,640]{2,1,0:T(8,128)} %get-tuple-element.9.refs_1_, f32[2,152,640]{2,1,0:T(8,128)} %get-tuple-element.10.refs_2_, ...), custom_call_target="tpu_custom_call" | custom-call | tf_op jit(solution)/shard_map/pallas_call | solution.py:930
